TPU v7x, 128 devices: a whole 4x4x4 slice. The times are simulated.
128 devices in a mesh: span: 8 (over z_lo, x), seq: 16 (over y, z_hi, core).
Axes of the slice: x: 4, y: 4, z: 4 (z_hi: 2, z_lo: 2; z = z_hi * 2 + z_lo), core: 2. Of those that a mesh axis runs over, the one named last changes fastest.
Arguments:
- queries: bfloat16 [16384, 4096], P(('span', 'seq')), may hold values from -120 to 120
- keys: bfloat16 [16384, 4096], P(('span', 'seq')), may hold values from -6 to 6
- values: bfloat16 [16384, 4096], P(('span', 'seq')), may hold values from -6 to 6
- out_grad: bfloat16 [16384, 4096], P(('span', 'seq')), may hold values from -6 to 6
- block_table: int32 [8, 8], replicated, may hold values from 0 to 1, as said below
Outputs:
- attended: bfloat16 [16384, 4096], P(('span', 'seq'))
- query_grad: bfloat16 [16384, 4096], P(('span', 'seq'))
- key_grad: bfloat16 [16384, 4096], P(('span', 'seq'))
- value_grad: bfloat16 [16384, 4096], P(('span', 'seq'))
Inputs may be any that keep to these rules, and one draw needn't show every extreme that they name: block_table[c, c] = 1; the other ones of row c stand only at columns c - 1 and c - 2; span 1 attends span 0, and span 2 attends span 0.
All inputs are finite; a program needn't handle non-finite values.
Results may differ from a plain program's by a relative error of at most 0.0051.
Values may be sent and summed in bfloat16 or wider, within the bound.
No kernel may reach another device: no remote copies, remote signals or barrier semaphores. Data moves between devices by JAX's collectives and lax.ppermute only.
A program may use at most 128 MiB of HBM per device.

v0:
```python
import math

import jax
import jax.numpy as jnp
from jax import lax
from jax.sharding import PartitionSpec as P

DH = 128


def passed_along(block, axis, distance):
    devices = range(lax.axis_size(axis))
    route = [(i - distance, i) for i in devices if i - distance in devices]
    return lax.ppermute(block, axis, route)


def score_sets(q_blk, key_sets, flags, scale):
    result = []
    for kk, flag in zip(key_sets, flags):
        item = jnp.einsum("qhd,khd->hqk", q_blk, kk, preferred_element_type=jnp.float32) * scale
        result.append(jnp.where(flag, item, jnp.float32(-1e30)))
    return result


def row_stats(s_list):
    top = jnp.max(s_list[0], -1)
    for item in s_list[1:]:
        top = jnp.maximum(top, jnp.max(item, -1))
    total = jnp.sum(jnp.exp(s_list[0] - top[..., None]), -1)
    for item in s_list[1:]:
        total = total + jnp.sum(jnp.exp(item - top[..., None]), -1)
    return (top, total)


def prob_sets(s_list, top, total):
    return [jnp.exp(item - top[..., None]) / total[..., None] for item in s_list]


def forward_values(p_list, val_sets):
    rounded = [item.astype(jnp.bfloat16) for item in p_list]
    acc = jnp.einsum("hqk,khd->qhd", rounded[0], val_sets[0], preferred_element_type=jnp.float32)
    for pb_item, vv in zip(rounded[1:], val_sets[1:]):
        acc = acc + jnp.einsum("hqk,khd->qhd", pb_item, vv, preferred_element_type=jnp.float32)
    return (rounded, acc.astype(jnp.bfloat16))


def backward_values(q_blk, g_blk, p_list, rounded, key_sets, val_sets, scale):
    dp_list = [
        jnp.einsum("qhd,khd->hqk", g_blk, vv, preferred_element_type=jnp.float32) for vv in val_sets
    ]
    delta = jnp.sum(p_list[0] * dp_list[0], -1)
    for pp, dd in zip(p_list[1:], dp_list[1:]):
        delta = delta + jnp.sum(pp * dd, -1)
    ds_list = [
        (pp * (dd - delta[..., None]) * scale).astype(jnp.bfloat16)
        for pp, dd in zip(p_list, dp_list)
    ]
    acc = jnp.einsum("hqk,khd->qhd", ds_list[0], key_sets[0], preferred_element_type=jnp.float32)
    for ds_item, kk in zip(ds_list[1:], key_sets[1:]):
        acc = acc + jnp.einsum("hqk,khd->qhd", ds_item, kk, preferred_element_type=jnp.float32)
    key_part = jnp.einsum("hqk,qhd->khd", ds_list[0], q_blk, preferred_element_type=jnp.float32)
    value_part = jnp.einsum("hqk,qhd->khd", rounded[0], g_blk, preferred_element_type=jnp.float32)
    return (acc.astype(jnp.bfloat16), key_part, value_part)


def body(queries, keys, values, out_grad, block_table):
    span_pos = lax.axis_index("span")
    near_use = jnp.where(span_pos >= 1, block_table[span_pos, jnp.maximum(span_pos - 1, 0)], 0) > 0
    far_use = jnp.where(span_pos >= 2, block_table[span_pos, jnp.maximum(span_pos - 2, 0)], 0) > 0
    q_h, k_h, v_h, g_h = (
        lax.all_to_all(queries, "seq", split_axis=1, concat_axis=0, tiled=True),
        lax.all_to_all(keys, "seq", split_axis=1, concat_axis=0, tiled=True),
        lax.all_to_all(values, "seq", split_axis=1, concat_axis=0, tiled=True),
        lax.all_to_all(out_grad, "seq", split_axis=1, concat_axis=0, tiled=True),
    )
    half = q_h.shape[0] // 2
    paired = jnp.stack([k_h[half:], v_h[half:]])
    near_pair = passed_along(paired, "span", 1)
    far_pair = passed_along(paired, "span", 2)
    nk_h, nv_h, fk_h, fv_h = (near_pair[0], near_pair[1], far_pair[0], far_pair[1])
    rows = q_h.shape[0]
    heads_here = q_h.shape[1] // DH
    scale = 1.0 / math.sqrt(DH)
    step = min(512, rows)
    count = rows // step
    q_view = q_h.reshape(rows, heads_here, DH)
    g_view = g_h.reshape(rows, heads_here, DH)
    key_sets = [
        k_h.reshape(rows, heads_here, DH),
        nk_h.reshape(half, heads_here, DH),
        fk_h.reshape(half, heads_here, DH),
    ]
    val_sets = [
        v_h.reshape(rows, heads_here, DH),
        nv_h.reshape(half, heads_here, DH),
        fv_h.reshape(half, heads_here, DH),
    ]
    flags = [jnp.bool_(True), near_use, far_use]
    zeros_bf = jnp.zeros((rows, heads_here, DH), jnp.bfloat16)
    zeros_f = jnp.zeros((rows, heads_here, DH), jnp.float32)

    def pick_rows(array, start):
        return lax.dynamic_slice_in_dim(array, start, step, 0)

    zeros_stat = jnp.zeros((heads_here, rows), jnp.float32)

    def forward_turn(index, carry):
        out_acc, top_acc, total_acc = carry
        start = index * step
        q_blk = pick_rows(q_view, start)
        s_list = score_sets(q_blk, key_sets, flags, scale)
        top, total = row_stats(s_list)
        p_list = prob_sets(s_list, top, total)
        rounded, out_blk = forward_values(p_list, val_sets)
        out_acc = lax.dynamic_update_slice_in_dim(out_acc, out_blk, start, 0)
        top_acc = lax.dynamic_update_slice_in_dim(top_acc, top, start, 1)
        total_acc = lax.dynamic_update_slice_in_dim(total_acc, total, start, 1)
        return (out_acc, top_acc, total_acc)

    out_h, top_all, total_all = lax.fori_loop(
        0, count, forward_turn, (zeros_bf, zeros_stat, zeros_stat)
    )
    attended = lax.all_to_all(
        out_h.reshape(rows, heads_here * DH), "seq", split_axis=0, concat_axis=1, tiled=True
    )

    def backward_turn(index, carry):
        dq_acc, dk_acc, dv_acc = carry
        start = index * step
        q_blk = pick_rows(q_view, start)
        g_blk = pick_rows(g_view, start)
        top = lax.dynamic_slice_in_dim(top_all, start, step, 1)
        total = lax.dynamic_slice_in_dim(total_all, start, step, 1)
        s_list = score_sets(q_blk, key_sets, flags, scale)
        p_list = prob_sets(s_list, top, total)
        rounded = [item.astype(jnp.bfloat16) for item in p_list]
        dq_blk, key_part, value_part = backward_values(
            q_blk, g_blk, p_list, rounded, key_sets, val_sets, scale
        )
        dq_acc = lax.dynamic_update_slice_in_dim(dq_acc, dq_blk, start, 0)
        return (dq_acc, dk_acc + key_part, dv_acc + value_part)

    dq_h, dk_sum, dv_sum = lax.fori_loop(0, count, backward_turn, (zeros_bf, zeros_f, zeros_f))
    query_grad, key_grad, value_grad = (
        lax.all_to_all(
            dq_h.reshape(rows, heads_here * DH), "seq", split_axis=0, concat_axis=1, tiled=True
        ),
        lax.all_to_all(
            dk_sum.astype(jnp.bfloat16).reshape(rows, heads_here * DH),
            "seq",
            split_axis=0,
            concat_axis=1,
            tiled=True,
        ),
        lax.all_to_all(
            dv_sum.astype(jnp.bfloat16).reshape(rows, heads_here * DH),
            "seq",
            split_axis=0,
            concat_axis=1,
            tiled=True,
        ),
    )
    return (attended, query_grad, key_grad, value_grad)


def solution(mesh):
    return jax.shard_map(
        body,
        mesh=mesh,
        in_specs=(
            P(("span", "seq"), None),
            P(("span", "seq"), None),
            P(("span", "seq"), None),
            P(("span", "seq"), None),
            P(),
        ),
        out_specs=(
            P(("span", "seq"), None),
            P(("span", "seq"), None),
            P(("span", "seq"), None),
            P(("span", "seq"), None),
        ),
        check_vma=False,
    )
```

profile of v0, /device:TPU:1, one launch (start us, length us, event | category | flops | bytes accessed | tf_op | source)
XLA Modules:
  0.0 477.9 jit_solution(12256258185556541398)
XLA Ops:
  3.1 9.3 %all-to-all-start.1 = ((bf16[128,16,256]{0,2,1:T(8,128)(2,1)}), bf16[128,16,256]{0,2,1:T(8,128)(2,1)S(1)}, u32[]{:S(2)}, u32[]{:S(2)}) async-start(bf16[128,16,256]{0,2,1:T(8,128)(2,1)} %bitcast.3), calls=%async_computation.1 | async-start | bytes 2097152 | tf_op jit(solution)/shard_map/all_to_all | solution.py:72
  13.7 15.9 %all-to-all-done.1 = bf16[128,16,256]{0,2,1:T(8,128)(2,1)S(1)} async-done(((bf16[128,16,256]{0,2,1:T(8,128)(2,1)}), bf16[128,16,256]{0,2,1:T(8,128)(2,1)S(1)}, u32[]{:S(2)}, u32[]{:S(2)}) %all-to-all-start.1) | async-done | bytes 1048608 | tf_op jit(solution)/shard_map/all_to_all | solution.py:72
  35.2 16.0 %all-to-all-done.2 = bf16[128,16,256]{0,2,1:T(8,128)(2,1)S(1)} async-done(((bf16[128,16,256]{0,2,1:T(8,128)(2,1)}), bf16[128,16,256]{0,2,1:T(8,128)(2,1)S(1)}, u32[]{:S(2)}, u32[]{:S(2)}) %all-to-all-start.2) | async-done | bytes 1048608 | tf_op jit(solution)/shard_map/all_to_all | solution.py:73
  72.8 5.0 %all-to-all-start.4 = ((bf16[128,16,256]{0,2,1:T(8,128)(2,1)}), bf16[128,16,256]{0,2,1:T(8,128)(2,1)}, u32[]{:S(2)}, u32[]{:S(2)}) async-start(bf16[128,16,256]{0,2,1:T(8,128)(2,1)} %bitcast.134), calls=%async_computation.4 | async-start | bytes 2097152 | tf_op jit(solution)/shard_map/all_to_all | solution.py:74
  77.8 5.6 %collective-permute-start.1 = (bf16[2,1024,256]{2,1,0:T(8,128)(2,1)}, bf16[2,1024,256]{2,1,0:T(8,128)(2,1)}, u32[]{:S(2)}, u32[]{:S(2)}) collective-permute-start(bf16[2,1024,256]{2,1,0:T(8,128)(2,1)} %pad_maximum_fusion), channel_id=1, source_target_pairs={{0,32},{16,48},{32,64},{48,80},{64,96},{80,112},{1,33},{17,49},{33... | collective-permute-start | bytes 3145736 | tf_op jit(solution)/shard_map/ppermute | solution.py:14
  99.5 30.0 %all-to-all-done.4 = bf16[128,16,256]{0,2,1:T(8,128)(2,1)} async-done(((bf16[128,16,256]{0,2,1:T(8,128)(2,1)}), bf16[128,16,256]{0,2,1:T(8,128)(2,1)}, u32[]{:S(2)}, u32[]{:S(2)}) %all-to-all-start.4) | async-done | bytes 1048608 | tf_op jit(solution)/shard_map/all_to_all | solution.py:74
  140.3 72.7 %while.35 = (s32[]{:T(128)}, bf16[2048,2,128]{0,2,1:T(8,128)(2,1)S(1)}, f32[2,2048]{1,0:T(2,128)S(1)}, f32[2,2048]{1,0:T(2,128)S(1)}, bf16[2048,2,128]{2,0,1:T(8...) while((s32[]{:T(128)}, ...), condition=%wide.region_7.8_spmd, body=%wide.region_0.7_spmd.sunk | while | flops 2191915008 | bytes 58819812 | solution.py:120
  214.3 170.4 %while.36 = (s32[]{:T(128)}, bf16[2048,2,128]{0,2,1:T(8,128)(2,1)}, f32[2048,2,128]{0,2,1:T(8,128)}, f32[2048,2,128]{0,2,1:T(8,128)}, bf16[2048,2,128]{2,0,1:T(8...) while((s32[]{:T(128)}, bf16[2048,2,128]{0,2,1:T(8,128)(2,1)}, ...), condition=%wide.region_12.13_spmd.clone, body=%wide.region_8.12_spmd.clone.sunk | while | flops 4339399680 | bytes 225789392 | solution.py:143
  223.2 5.1 %multiply_reduce_fusion.10 = (f32[2,512]{1,0:T(2,128)S(1)}, f32[2,512,1024]{2,1,0:T(8,128)}) fusion(f32[2,512,1024]{2,1,0:T(8,128)S(1)} %fusion.156, f32[2,512]{1,0:T(2,128)S(1)} %get-tuple-element.958, f32[2,512]{1,0:T(2,128)S(1)} %get-tuple-element.959, bf16[1024,2,128]{2,0,1:T(8,128)(2,1)} %get-tuple-element.1071, ...), kind=kOutput, calls=%fused_computation.47.clone.1 | convolution fusion | flops 274725888 | bytes 9187844 | tf_op jit(solution)/shard_map/while/body/eval_jaxpr/qhd,khd->hqk/dot_general | solution.py:20
  230.2 4.6 multiply_reduce_fusion.11
  250.1 6.3 %fusion.162 = f32[2048,2,128]{0,2,1:T(8,128)} fusion(f32[2,512,2048]{2,1,0:T(8,128)} %copy-done.1, f32[2048,2,128]{0,2,1:T(8,128)} %get-tuple-element.1040, pred[]{:T(512)S(6)} %compare.3, bf16[2048,2,128]{0,2,1:T(8,128)(2,1)} %get-tuple-element.1065, s32[]{:T(128)S(6)} %select_n.169), kind=kOutput, calls=%fused_computation.54.clone.1 | convolution fusion | flops 540016640 | bytes 12845061 | tf_op jit(solution)/shard_map/while/body/eval_jaxpr/hqk,qhd->khd/dot_general | solution.py:62
  265.4 5.1 %multiply_reduce_fusion.10 = (f32[2,512]{1,0:T(2,128)S(1)}, f32[2,512,1024]{2,1,0:T(8,128)}) fusion(f32[2,512,1024]{2,1,0:T(8,128)S(1)} %fusion.156, f32[2,512]{1,0:T(2,128)S(1)} %get-tuple-element.958, f32[2,512]{1,0:T(2,128)S(1)} %get-tuple-element.959, bf16[1024,2,128]{2,0,1:T(8,128)(2,1)} %get-tuple-element.1071, ...), kind=kOutput, calls=%fused_computation.47.clone.1 | convolution fusion | flops 274725888 | bytes 9187844 | tf_op jit(solution)/shard_map/while/body/eval_jaxpr/qhd,khd->hqk/dot_general | solution.py:20
  272.3 4.6 multiply_reduce_fusion.11
  292.3 6.9 %fusion.162 = f32[2048,2,128]{0,2,1:T(8,128)} fusion(f32[2,512,2048]{2,1,0:T(8,128)} %copy-done.1, f32[2048,2,128]{0,2,1:T(8,128)} %get-tuple-element.1040, pred[]{:T(512)S(6)} %compare.3, bf16[2048,2,128]{0,2,1:T(8,128)(2,1)} %get-tuple-element.1065, s32[]{:T(128)S(6)} %select_n.169), kind=kOutput, calls=%fused_computation.54.clone.1 | convolution fusion | flops 540016640 | bytes 12845061 | tf_op jit(solution)/shard_map/while/body/eval_jaxpr/hqk,qhd->khd/dot_general | solution.py:62
  308.1 5.1 %multiply_reduce_fusion.10 = (f32[2,512]{1,0:T(2,128)S(1)}, f32[2,512,1024]{2,1,0:T(8,128)}) fusion(f32[2,512,1024]{2,1,0:T(8,128)S(1)} %fusion.156, f32[2,512]{1,0:T(2,128)S(1)} %get-tuple-element.958, f32[2,512]{1,0:T(2,128)S(1)} %get-tuple-element.959, bf16[1024,2,128]{2,0,1:T(8,128)(2,1)} %get-tuple-element.1071, ...), kind=kOutput, calls=%fused_computation.47.clone.1 | convolution fusion | flops 274725888 | bytes 9187844 | tf_op jit(solution)/shard_map/while/body/eval_jaxpr/qhd,khd->hqk/dot_general | solution.py:20
  335.0 6.9 %fusion.162 = f32[2048,2,128]{0,2,1:T(8,128)} fusion(f32[2,512,2048]{2,1,0:T(8,128)} %copy-done.1, f32[2048,2,128]{0,2,1:T(8,128)} %get-tuple-element.1040, pred[]{:T(512)S(6)} %compare.3, bf16[2048,2,128]{0,2,1:T(8,128)(2,1)} %get-tuple-element.1065, s32[]{:T(128)S(6)} %select_n.169), kind=kOutput, calls=%fused_computation.54.clone.1 | convolution fusion | flops 540016640 | bytes 12845061 | tf_op jit(solution)/shard_map/while/body/eval_jaxpr/hqk,qhd->khd/dot_general | solution.py:62
  350.8 5.1 %multiply_reduce_fusion.10 = (f32[2,512]{1,0:T(2,128)S(1)}, f32[2,512,1024]{2,1,0:T(8,128)}) fusion(f32[2,512,1024]{2,1,0:T(8,128)S(1)} %fusion.156, f32[2,512]{1,0:T(2,128)S(1)} %get-tuple-element.958, f32[2,512]{1,0:T(2,128)S(1)} %get-tuple-element.959, bf16[1024,2,128]{2,0,1:T(8,128)(2,1)} %get-tuple-element.1071, ...), kind=kOutput, calls=%fused_computation.47.clone.1 | convolution fusion | flops 274725888 | bytes 9187844 | tf_op jit(solution)/shard_map/while/body/eval_jaxpr/qhd,khd->hqk/dot_general | solution.py:20
  377.8 6.9 %fusion.162 = f32[2048,2,128]{0,2,1:T(8,128)} fusion(f32[2,512,2048]{2,1,0:T(8,128)} %copy-done.1, f32[2048,2,128]{0,2,1:T(8,128)} %get-tuple-element.1040, pred[]{:T(512)S(6)} %compare.3, bf16[2048,2,128]{0,2,1:T(8,128)(2,1)} %get-tuple-element.1065, s32[]{:T(128)S(6)} %select_n.169), kind=kOutput, calls=%fused_computation.54.clone.1 | convolution fusion | flops 540016640 | bytes 12845061 | tf_op jit(solution)/shard_map/while/body/eval_jaxpr/hqk,qhd->khd/dot_general | solution.py:62
  388.2 4.6 all-to-all-start.6
  396.5 13.6 %all-to-all-done.6 = bf16[16,128,256]{2,1,0:T(8,128)(2,1)S(1)} async-done(((bf16[16,128,256]{2,1,0:T(8,128)(2,1)}), bf16[16,128,256]{2,1,0:T(8,128)(2,1)S(1)}, u32[]{:S(2)}, u32[]{:S(2)}) %all-to-all-start.6) | async-done | bytes 1048608 | tf_op jit(solution)/shard_map/all_to_all | solution.py:148
  415.9 15.8 %all-to-all-done.7 = bf16[16,128,256]{2,1,0:T(8,128)(2,1)S(1)} async-done(((bf16[16,128,256]{2,1,0:T(8,128)(2,1)}), bf16[16,128,256]{2,1,0:T(8,128)(2,1)S(1)}, u32[]{:S(2)}, u32[]{:S(2)}) %all-to-all-start.7) | async-done | bytes 1048608 | tf_op jit(solution)/shard_map/all_to_all | solution.py:155
  438.7 14.6 %all-to-all-done.5 = bf16[16,128,256]{1,2,0:T(8,128)(2,1)S(1)} async-done(((bf16[16,128,256]{1,2,0:T(8,128)(2,1)}), bf16[16,128,256]{1,2,0:T(8,128)(2,1)S(1)}, u32[]{:S(2)}, u32[]{:S(2)}) %all-to-all-start.5) | async-done | bytes 1048608 | tf_op jit(solution)/shard_map/all_to_all | solution.py:145
  453.3 4.9 %all-to-all-start.3 = ((bf16[16,128,256]{1,2,0:T(8,128)(2,1)}), bf16[16,128,256]{1,2,0:T(8,128)(2,1)}, u32[]{:S(2)}, u32[]{:S(2)}) async-start(bf16[16,128,256]{1,2,0:T(8,128)(2,1)} %copy.140), calls=%async_computation.3 | async-start | bytes 2097152 | tf_op jit(solution)/shard_map/all_to_all | solution.py:123
  465.1 10.5 %all-to-all-done.3 = bf16[16,128,256]{1,2,0:T(8,128)(2,1)} async-done(((bf16[16,128,256]{1,2,0:T(8,128)(2,1)}), bf16[16,128,256]{1,2,0:T(8,128)(2,1)}, u32[]{:S(2)}, u32[]{:S(2)}) %all-to-all-start.3) | async-done | bytes 1048608 | tf_op jit(solution)/shard_map/all_to_all | solution.py:123
  (225 shorter events, 272.4 us)
Async XLA Ops:
  0.6 11.7 %copy-start.11 = (bf16[128,4096]{1,0:T(8,128)(2,1)S(1)}, bf16[128,4096]{1,0:T(8,128)(2,1)}, u32[]{:S(2)}) copy-start(bf16[128,4096]{1,0:T(8,128)(2,1)} %param.11) | copy-start | bytes 3145732
  0.6 33.2 %copy-start.12 = (bf16[128,4096]{1,0:T(8,128)(2,1)S(1)}, bf16[128,4096]{1,0:T(8,128)(2,1)}, u32[]{:S(2)}) copy-start(bf16[128,4096]{1,0:T(8,128)(2,1)} %param.9) | copy-start | bytes 3145732
  3.1 26.5 %all-to-all-start.1 = ((bf16[128,16,256]{0,2,1:T(8,128)(2,1)}), bf16[128,16,256]{0,2,1:T(8,128)(2,1)S(1)}, u32[]{:S(2)}, u32[]{:S(2)}) async-start(bf16[128,16,256]{0,2,1:T(8,128)(2,1)} %bitcast.3), calls=%async_computation.1 | async-start | bytes 2097152 | tf_op jit(solution)/shard_map/all_to_all | solution.py:72
  29.6 21.6 %all-to-all-start.2 = ((bf16[128,16,256]{0,2,1:T(8,128)(2,1)}), bf16[128,16,256]{0,2,1:T(8,128)(2,1)S(1)}, u32[]{:S(2)}, u32[]{:S(2)}) async-start(bf16[128,16,256]{0,2,1:T(8,128)(2,1)} %bitcast.7), calls=%async_computation.2 | async-start | bytes 2097152 | tf_op jit(solution)/shard_map/all_to_all | solution.py:73
  51.2 21.6 %all-to-all-start = ((bf16[128,16,256]{0,2,1:T(8,128)(2,1)}), bf16[128,16,256]{0,2,1:T(8,128)(2,1)S(1)}, u32[]{:S(2)}, u32[]{:S(2)}) async-start(bf16[128,16,256]{0,2,1:T(8,128)(2,1)} %bitcast.136), calls=%async_computation | async-start | bytes 2097152 | tf_op jit(solution)/shard_map/all_to_all | solution.py:71
  63.5 69.2 %collective-permute-start = (bf16[2,1024,256]{2,1,0:T(8,128)(2,1)}, bf16[2,1024,256]{2,1,0:T(8,128)(2,1)}, u32[]{:S(2)}, u32[]{:S(2)}) collective-permute-start(bf16[2,1024,256]{2,1,0:T(8,128)(2,1)} %pad_maximum_fusion), channel_id=1, source_target_pairs={{0,16},{16,32},{32,48},{48,64},{64,80},{80,96},{96,112},{1,17},{17... | collective-permute-start | bytes 3145736 | tf_op jit(solution)/shard_map/ppermute | solution.py:14
  72.8 16.5 %copy-start.6 = (bf16[128,16,256]{0,2,1:T(8,128)(2,1)}, bf16[128,16,256]{0,2,1:T(8,128)(2,1)S(1)}, u32[]{:S(2)}) copy-start(bf16[128,16,256]{0,2,1:T(8,128)(2,1)S(1)} %all-to-all-done) | copy-start | bytes 3145732
  72.8 56.7 %all-to-all-start.4 = ((bf16[128,16,256]{0,2,1:T(8,128)(2,1)}), bf16[128,16,256]{0,2,1:T(8,128)(2,1)}, u32[]{:S(2)}, u32[]{:S(2)}) async-start(bf16[128,16,256]{0,2,1:T(8,128)(2,1)} %bitcast.134), calls=%async_computation.4 | async-start | bytes 2097152 | tf_op jit(solution)/shard_map/all_to_all | solution.py:74
  77.8 57.4 %collective-permute-start.1 = (bf16[2,1024,256]{2,1,0:T(8,128)(2,1)}, bf16[2,1024,256]{2,1,0:T(8,128)(2,1)}, u32[]{:S(2)}, u32[]{:S(2)}) collective-permute-start(bf16[2,1024,256]{2,1,0:T(8,128)(2,1)} %pad_maximum_fusion), channel_id=1, source_target_pairs={{0,32},{16,48},{32,64},{48,80},{64,96},{80,112},{1,33},{17,49},{33... | collective-permute-start | bytes 3145736 | tf_op jit(solution)/shard_map/ppermute | solution.py:14
  220.7 14.1 %copy-start.1 = (f32[2,512,2048]{2,1,0:T(8,128)}, f32[2,512,2048]{2,1,0:T(8,128)S(1)}, u32[]{:S(2)}) copy-start(f32[2,512,2048]{2,1,0:T(8,128)S(1)} %get-tuple-element.960) | copy-start | bytes 25165828 | tf_op jit(solution)/shard_map/while
  250.1 6.3 %copy-start.5 = (f32[2048,2,128]{0,2,1:T(8,128)}, f32[2048,2,128]{0,2,1:T(8,128)S(1)}, u32[]{:S(2)}) copy-start(f32[2048,2,128]{0,2,1:T(8,128)S(1)} %fusion.161) | copy-start | bytes 6291460 | tf_op jit(solution)/shard_map/while
  262.9 14.1 %copy-start.1 = (f32[2,512,2048]{2,1,0:T(8,128)}, f32[2,512,2048]{2,1,0:T(8,128)S(1)}, u32[]{:S(2)}) copy-start(f32[2,512,2048]{2,1,0:T(8,128)S(1)} %get-tuple-element.960) | copy-start | bytes 25165828 | tf_op jit(solution)/shard_map/while
  278.0 5.8 %copy-start = (bf16[2,512,2048]{2,1,0:T(8,128)(2,1)}, bf16[2,512,2048]{2,1,0:T(8,128)(2,1)S(1)}, u32[]{:S(2)}) copy-start(bf16[2,512,2048]{2,1,0:T(8,128)(2,1)S(1)} %multiply_convert_fusion.18) | copy-start | bytes 12582916 | tf_op jit(solution)/shard_map/while
  292.3 6.9 %copy-start.5 = (f32[2048,2,128]{0,2,1:T(8,128)}, f32[2048,2,128]{0,2,1:T(8,128)S(1)}, u32[]{:S(2)}) copy-start(f32[2048,2,128]{0,2,1:T(8,128)S(1)} %fusion.161) | copy-start | bytes 6291460 | tf_op jit(solution)/shard_map/while
  305.6 14.1 %copy-start.1 = (f32[2,512,2048]{2,1,0:T(8,128)}, f32[2,512,2048]{2,1,0:T(8,128)S(1)}, u32[]{:S(2)}) copy-start(f32[2,512,2048]{2,1,0:T(8,128)S(1)} %get-tuple-element.960) | copy-start | bytes 25165828 | tf_op jit(solution)/shard_map/while
  320.8 5.8 %copy-start = (bf16[2,512,2048]{2,1,0:T(8,128)(2,1)}, bf16[2,512,2048]{2,1,0:T(8,128)(2,1)S(1)}, u32[]{:S(2)}) copy-start(bf16[2,512,2048]{2,1,0:T(8,128)(2,1)S(1)} %multiply_convert_fusion.18) | copy-start | bytes 12582916 | tf_op jit(solution)/shard_map/while
  335.0 6.9 %copy-start.5 = (f32[2048,2,128]{0,2,1:T(8,128)}, f32[2048,2,128]{0,2,1:T(8,128)S(1)}, u32[]{:S(2)}) copy-start(f32[2048,2,128]{0,2,1:T(8,128)S(1)} %fusion.161) | copy-start | bytes 6291460 | tf_op jit(solution)/shard_map/while
  348.4 14.1 %copy-start.1 = (f32[2,512,2048]{2,1,0:T(8,128)}, f32[2,512,2048]{2,1,0:T(8,128)S(1)}, u32[]{:S(2)}) copy-start(f32[2,512,2048]{2,1,0:T(8,128)S(1)} %get-tuple-element.960) | copy-start | bytes 25165828 | tf_op jit(solution)/shard_map/while
  377.7 6.9 %copy-start.5 = (f32[2048,2,128]{0,2,1:T(8,128)}, f32[2048,2,128]{0,2,1:T(8,128)S(1)}, u32[]{:S(2)}) copy-start(f32[2048,2,128]{0,2,1:T(8,128)S(1)} %fusion.161) | copy-start | bytes 6291460 | tf_op jit(solution)/shard_map/while
  388.2 21.8 %all-to-all-start.6 = ((bf16[16,128,256]{2,1,0:T(8,128)(2,1)}), bf16[16,128,256]{2,1,0:T(8,128)(2,1)S(1)}, u32[]{:S(2)}, u32[]{:S(2)}) async-start(bf16[16,128,256]{2,1,0:T(8,128)(2,1)} %copy.163), calls=%async_computation.6 | async-start | bytes 2097152 | tf_op jit(solution)/shard_map/all_to_all | solution.py:148
  392.8 21.5 %copy-start.9 = (bf16[2048,2,128]{0,2,1:T(8,128)(2,1)S(1)}, bf16[2048,2,128]{0,2,1:T(8,128)(2,1)}, u32[]{:S(2)}) copy-start(bf16[2048,2,128]{0,2,1:T(8,128)(2,1)} %get-tuple-element.484) | copy-start | bytes 3145732
  410.1 21.6 %all-to-all-start.7 = ((bf16[16,128,256]{2,1,0:T(8,128)(2,1)}), bf16[16,128,256]{2,1,0:T(8,128)(2,1)S(1)}, u32[]{:S(2)}, u32[]{:S(2)}) async-start(bf16[16,128,256]{2,1,0:T(8,128)(2,1)} %copy.164), calls=%async_computation.7 | async-start | bytes 2097152 | tf_op jit(solution)/shard_map/all_to_all | solution.py:155
  431.7 21.6 %all-to-all-start.5 = ((bf16[16,128,256]{1,2,0:T(8,128)(2,1)}), bf16[16,128,256]{1,2,0:T(8,128)(2,1)S(1)}, u32[]{:S(2)}, u32[]{:S(2)}) async-start(bf16[16,128,256]{1,2,0:T(8,128)(2,1)} %copy.152), calls=%async_computation.5 | async-start | bytes 2097152 | tf_op jit(solution)/shard_map/all_to_all | solution.py:145
  453.3 22.3 %all-to-all-start.3 = ((bf16[16,128,256]{1,2,0:T(8,128)(2,1)}), bf16[16,128,256]{1,2,0:T(8,128)(2,1)}, u32[]{:S(2)}, u32[]{:S(2)}) async-start(bf16[16,128,256]{1,2,0:T(8,128)(2,1)} %copy.140), calls=%async_computation.3 | async-start | bytes 2097152 | tf_op jit(solution)/shard_map/all_to_all | solution.py:123
  (17 other events, 65.4 us)
where the time goes:
time: 481 us; the launch traced here: 478 us
  matrix products  201 us (42%)
  waiting for transfers between devices  119 us (25%)
  local copies, waits for them, and re-layouts  78.6 us (16%)
  starting transfers between devices  50.8 us (11%)
  other arithmetic  24.7 us (5%)
    dot_general x24, matrix products, score_sets(): jnp.einsum('qhd,khd->hqk', q_blk, kk, preferred_element_type=jnp.float32)  78.6 us
    all_to_all x1, waiting for transfers between devices, body(): lax.all_to_all(out_grad, 'seq', split_axis=1, concat_axis=0, tiled=True)  30 us
    dot_general x12, matrix products, backward_values(): jnp.einsum('qhd,khd->hqk', g_blk, vv, preferred_element_type=jnp.float32)  27.9 us
    dot_general x4, matrix products, backward_values(): jnp.einsum('hqk,qhd->khd', rounded[0], g_blk, preferred_element_type=jnp....  27 us
    dot_general x8, matrix products, forward_values(): jnp.einsum('hqk,khd->qhd', pb_item, vv, preferred_element_type=jnp.float32)  17.9 us
    dot_general x8, matrix products, backward_values(): jnp.einsum('hqk,khd->qhd', ds_item, kk, preferred_element_type=jnp.float32)  16.8 us
    unnamed x26, local copies, waits for them, and re-layouts  16.7 us
    all_to_all x1, waiting for transfers between devices, body(): lax.all_to_all(values, 'seq', split_axis=1, concat_axis=0, tiled=True)  16 us
  transfers between devices with their start and end apart: 10, of which 8 were waited for; matrix products, arithmetic and copies ran while one was open for 10% of the time, Pallas kernels for 0%

commit v1 on v0

v1 whole, which is shorter than its diff:
```python
import functools
import math

import jax
import jax.numpy as jnp
from jax import lax
from jax.experimental import pallas as pl
from jax.experimental.pallas import tpu as pltpu
from jax.sharding import PartitionSpec as P

DH = 128
F32 = jnp.float32
BF16 = jnp.bfloat16
SCALE = 1.0 / math.sqrt(DH)
SCALE2 = SCALE * math.log2(math.e)
NT = (((1,), (1,)), ((), ()))
NN = (((1,), (0,)), ((), ()))
TN = (((0,), (0,)), ((), ()))
VMEM_LIMIT = 56 * 2**20


def dot(a, b, dims):
    return lax.dot_general(a, b, dims, preferred_element_type=F32)


def fold(op, x):
    result = x[:, :DH]
    for i in range(DH, x.shape[1], DH):
        result = op(result, x[:, i : i + DH])
    return result


def attention_kernel(
    q_rows, k_cols, flags_ref, x_ref, near_ref, far_ref, out_ref, k_s, v_s, s_s, dp_s, dk_s, dv_s
):
    rows = x_ref.shape[0] * DH
    half = near_ref.shape[0] * DH
    near, far = flags_ref[0], flags_ref[1]
    k_s[:rows] = x_ref[:, 0].reshape(rows, DH)
    v_s[:rows] = x_ref[:, 1].reshape(rows, DH)

    @pl.when(near > 0)
    def _():
        k_s[rows : rows + half] = near_ref[:, 0].reshape(half, DH)
        v_s[rows : rows + half] = near_ref[:, 1].reshape(half, DH)

    @pl.when(far > 0)
    def _():
        start = pl.multiple_of(rows + near * half, half)
        k_s[pl.ds(start, half)] = far_ref[:, 0].reshape(half, DH)
        v_s[pl.ds(start, half)] = far_ref[:, 1].reshape(half, DH)

    dk_s[...] = jnp.zeros_like(dk_s)
    dv_s[...] = jnp.zeros_like(dv_s)
    group = q_rows // DH

    def run(contexts):
        chunks = range(0, rows + contexts * half, k_cols)

        def block(i, carry):
            here = pl.ds(i * group, group)
            q = x_ref[here, 2].reshape(q_rows, DH)
            g = x_ref[here, 3].reshape(q_rows, DH)
            top = None
            for c in chunks:
                s = dot(q, k_s[c : c + k_cols], NT)
                s_s[:, c : c + k_cols] = s
                part = fold(jnp.maximum, s)
                top = part if top is None else jnp.maximum(top, part)
            top = jnp.max(top, 1, keepdims=True) * SCALE2
            total = delta = out = None
            for c in chunks:
                e = jnp.exp2(s_s[:, c : c + k_cols] * SCALE2 - top)
                s_s[:, c : c + k_cols] = e
                dp = dot(g, v_s[c : c + k_cols], NT)
                dp_s[:, c : c + k_cols] = dp
                t_part, d_part = fold(jnp.add, e), fold(jnp.add, e * dp)
                o_part = dot(e.astype(BF16), v_s[c : c + k_cols], NN)
                total = t_part if total is None else total + t_part
                delta = d_part if delta is None else delta + d_part
                out = o_part if out is None else out + o_part
            inv = 1.0 / jnp.sum(total, 1, keepdims=True)
            delta = jnp.sum(delta, 1, keepdims=True) * inv
            out_ref[here, 0] = (out * inv).astype(BF16).reshape(group, DH, DH)
            g_over = (g.astype(F32) * inv).astype(BF16)
            q_over = (q.astype(F32) * (inv * SCALE)).astype(BF16)
            dq = None
            for c in chunks:
                e = s_s[:, c : c + k_cols]
                ds = (e * (dp_s[:, c : c + k_cols] - delta)).astype(BF16)
                part = dot(ds, k_s[c : c + k_cols], NN)
                dq = part if dq is None else dq + part
                if c < rows:
                    dk_s[c : c + k_cols] += dot(ds, q_over, TN)
                    dv_s[c : c + k_cols] += dot(e.astype(BF16), g_over, TN)
            out_ref[here, 1] = (dq * (inv * SCALE)).astype(BF16).reshape(group, DH, DH)
            return carry

        lax.fori_loop(0, rows // q_rows, block, 0)

    for contexts in range(3):
        pl.when(near + far == contexts)(functools.partial(run, contexts))
    out_ref[:, 2] = dk_s[...].astype(BF16).reshape(rows // DH, DH, DH)
    out_ref[:, 3] = dv_s[...].astype(BF16).reshape(rows // DH, DH, DH)


def attention(flags, x, near, far, q_rows=256, k_cols=1024):
    rows, half = x.shape[0] * DH, near.shape[0] * DH
    length = rows + 2 * half
    vmem = pl.BlockSpec(memory_space=pltpu.VMEM)
    return pl.pallas_call(
        functools.partial(attention_kernel, q_rows, k_cols),
        out_shape=jax.ShapeDtypeStruct(x.shape, BF16),
        in_specs=[pl.BlockSpec(memory_space=pltpu.SMEM), vmem, vmem, vmem],
        out_specs=vmem,
        scratch_shapes=[
            pltpu.VMEM((length, DH), BF16),
            pltpu.VMEM((length, DH), BF16),
            pltpu.VMEM((q_rows, length), F32),
            pltpu.VMEM((q_rows, length), F32),
            pltpu.VMEM((rows, DH), F32),
            pltpu.VMEM((rows, DH), F32),
        ],
        compiler_params=pltpu.CompilerParams(vmem_limit_bytes=VMEM_LIMIT),
        cost_estimate=pl.CostEstimate(
            flops=40 * 10**9, bytes_accessed=6 * 2**20, transcendentals=rows * length
        ),
        name="attention",
    )(flags, x, near, far)


def pack_kernel(k_ref, v_ref, q_ref, g_ref, a_ref, b_ref):
    for j in range(a_ref.shape[0]):
        for i, ref in enumerate((k_ref, v_ref, q_ref, g_ref)):
            a_ref[j, i] = ref[:, 2 * j * DH : (2 * j + 1) * DH]
            b_ref[j, i] = ref[:, (2 * j + 1) * DH : (2 * j + 2) * DH]


def pack(arrays):
    tokens, width = arrays[0].shape
    dests = width // (2 * DH)
    step = 4
    shape = jax.ShapeDtypeStruct((dests, 4, tokens, DH), BF16)
    return pl.pallas_call(
        pack_kernel,
        grid=(dests // step,),
        out_shape=(shape, shape),
        in_specs=[pl.BlockSpec((tokens, step * 2 * DH), lambda j: (0, j))] * 4,
        out_specs=[pl.BlockSpec((step, 4, tokens, DH), lambda j: (j, 0, 0, 0))] * 2,
        cost_estimate=pl.CostEstimate(flops=0, bytes_accessed=8 * 2**20, transcendentals=0),
        name="pack",
    )(*arrays)


def unpack_kernel(a_ref, b_ref, *out_refs):
    for j in range(a_ref.shape[0]):
        for i, ref in enumerate(out_refs):
            ref[:, 2 * j * DH : (2 * j + 1) * DH] = a_ref[j, i]
            ref[:, (2 * j + 1) * DH : (2 * j + 2) * DH] = b_ref[j, i]


def unpack(a, b):
    sources, _, tokens, _ = a.shape
    step = 4
    shape = jax.ShapeDtypeStruct((tokens, sources * 2 * DH), BF16)
    return pl.pallas_call(
        unpack_kernel,
        grid=(sources // step,),
        out_shape=(shape,) * 4,
        in_specs=[pl.BlockSpec((step, 4, tokens, DH), lambda j: (j, 0, 0, 0))] * 2,
        out_specs=[pl.BlockSpec((tokens, step * 2 * DH), lambda j: (0, j))] * 4,
        cost_estimate=pl.CostEstimate(flops=0, bytes_accessed=8 * 2**20, transcendentals=0),
        name="unpack",
    )(a, b)


def passed_along(block, axis, distance):
    devices = range(lax.axis_size(axis))
    route = [(i - distance, i) for i in devices if i - distance in devices]
    return lax.ppermute(block, axis, route)


def exchange(block):
    return lax.all_to_all(block, "seq", split_axis=0, concat_axis=0, tiled=True)


def body(queries, keys, values, out_grad, block_table):
    span = lax.axis_index("span")
    near = jnp.where(span >= 1, block_table[span, jnp.maximum(span - 1, 0)], 0) > 0
    far = jnp.where(span >= 2, block_table[span, jnp.maximum(span - 2, 0)], 0) > 0
    flags = jnp.stack([near, far]).astype(jnp.int32)
    results = []
    for packed in pack((keys, values, queries, out_grad)):
        x = exchange(packed)
        tail = x[x.shape[0] // 2 :, :2]
        y = attention(flags, x, passed_along(tail, "span", 1), passed_along(tail, "span", 2))
        results.append(exchange(y))
    attended, query_grad, key_grad, value_grad = unpack(*results)
    return (attended, query_grad, key_grad, value_grad)


def solution(mesh):
    rows = P(("span", "seq"), None)
    return jax.shard_map(
        body,
        mesh=mesh,
        in_specs=(rows, rows, rows, rows, P()),
        out_specs=(rows, rows, rows, rows),
        check_vma=False,
    )
```

time: 481 us -> 219 us (0.46)
  matrix products: 201 us -> 0 us
  local copies, waits for them, and re-layouts: 78.6 us -> 2.47 us
  blocking collectives: 0 us -> 71.1 us
  Pallas kernels: 0 us -> 55.1 us
  waiting for transfers between devices: 119 us -> 64.4 us
  starting transfers between devices: 50.8 us -> 22.5 us
  other arithmetic: 24.7 us -> 0.59 us
    dot_general x68 -> x0, matrix products: 201 us -> none  [the longest x24 78.6 us: score_sets(): jnp.einsum('qhd,khd->hqk', q_blk, kk, preferred_element_type=jnp.float32)]
    all_to_all x0 -> x2, blocking collectives: none -> 71.1 us  [exchange(): return lax.all_to_all(block, 'seq', split_axis=0, concat_axis=0, tiled=True)]
    pallas_call x0 -> x4, Pallas kernels: none -> 55.1 us  [the longest x2 45.2 us: attention(): pl.pallas_call(functools.partial(attention_kernel, q_rows, k_cols), out_s...]
    all_to_all x8 -> x2, waiting for transfers between devices: 119 us -> 64.4 us  [exchange(): return lax.all_to_all(block, 'seq', split_axis=0, concat_axis=0, tiled=True)]
    all_to_all x8 -> x2, starting transfers between devices: 41.1 us -> 9.83 us  [exchange(): return lax.all_to_all(block, 'seq', split_axis=0, concat_axis=0, tiled=True)]
    while x55 -> x0, local copies, waits for them, and re-layouts: 20.3 us -> none
    unnamed x26 -> x4, local copies, waits for them, and re-layouts: 16.7 us -> 0.01 us
    reduce_sum x8 -> x0, other arithmetic: 14.2 us -> none  [the longest x4 7.65 us: row_stats(): total = total + jnp.sum(jnp.exp(item - top[..., None]), -1)]
  transfers between devices with their start and end apart: 10 -> 6, of which waited for: 8 -> 2; matrix products, arithmetic and copies ran while one was open for 10% -> 1% of each run, Pallas kernels for 0% -> 21%
where the time goes in v1:
time: 219 us; the launch traced here: 218 us
  blocking collectives  71.1 us (32%)
  waiting for transfers between devices  64.4 us (29%)
  Pallas kernels  55.1 us (25%)
  starting transfers between devices  22.5 us (10%)
  local copies, waits for them, and re-layouts  2.47 us (1%)
    all_to_all x2, blocking collectives, exchange(): return lax.all_to_all(block, 'seq', split_axis=0, concat_axis=0, tiled=True)  71.1 us
    all_to_all x2, waiting for transfers between devices, exchange(): return lax.all_to_all(block, 'seq', split_axis=0, concat_axis=0, tiled=True)  64.4 us
    pallas_call x2, Pallas kernels, attention(): pl.pallas_call(functools.partial(attention_kernel, q_rows, k_cols), out_s...  45.2 us
    ppermute x4, starting transfers between devices, passed_along(): return lax.ppermute(block, axis, route)  12.7 us
    all_to_all x2, starting transfers between devices, exchange(): return lax.all_to_all(block, 'seq', split_axis=0, concat_axis=0, tiled=True)  9.83 us
    pallas_call x1, Pallas kernels, unpack(): pl.pallas_call(unpack_kernel, grid=(sources // step,), out_shape=(shape,)...  5.05 us
    pallas_call x1, Pallas kernels, pack(): pl.pallas_call(pack_kernel, grid=(dests // step,), out_shape=(shape, shap...  4.89 us
  transfers between devices with their start and end apart: 6, of which 2 were waited for; matrix products, arithmetic and copies ran while one was open for 1% of the time, Pallas kernels for 21%

profile of v1, /device:TPU:1, one launch (start us, length us, event | category | flops | bytes accessed | tf_op | source)
XLA Modules:
  0.0 218.2 jit_solution(1384435883285512313)
XLA Ops:
  0.6 4.9 %pack.1 = (bf16[16,4,128,128]{3,2,1,0:T(8,128)(2,1)}, bf16[16,4,128,128]{3,2,1,0:T(8,128)(2,1)}) custom-call(bf16[128,4096]{1,0:T(8,128)(2,1)} %k_ref.1, bf16[128,4096]{1,0:T(8,128)(2,1)} %v_ref.1, bf16[128,4096]{1,0:T(8,128)(2,1)} %q_ref.1, bf16[128,4096]{1,0:T(8,128)(2,1)} %g_ref.1), custom_call_target="tpu_custom_call" | custom-call | bytes 8388608 | tf_op jit(solution)/shard_map/pack/pallas_call | solution.py:144
  5.5 37.4 %all_to_all.20.x_ref = bf16[16,4,128,128]{3,2,1,0:T(8,128)(2,1)} all-to-all(bf16[16,4,128,128]{3,2,1,0:T(8,128)(2,1)} %get-tuple-element.6), channel_id=1, replica_groups=mesh['span'=8,'seq'=16] {'seq'}, dimensions={0} | all-to-all | bytes 4194304 | tf_op jit(solution)/shard_map/all_to_all | solution.py:184
  42.9 4.8 %all-to-all-start.2 = ((bf16[16,4,128,128]{3,2,1,0:T(8,128)(2,1)}), bf16[16,4,128,128]{3,2,1,0:T(8,128)(2,1)S(1)}, u32[]{:S(2)}, u32[]{:S(2)}) async-start(bf16[16,4,128,128]{3,2,1,0:T(8,128)(2,1)} %get-tuple-element.7), calls=%async_computation.2 | async-start | bytes 4194304 | tf_op jit(solution)/shard_map/all_to_all | solution.py:184
  47.7 1.1 slice.8
  48.8 5.5 %collective-permute-start.1 = (bf16[8,2,128,128]{3,2,1,0:T(8,128)(2,1)S(1)}, bf16[8,2,128,128]{3,2,1,0:T(8,128)(2,1)}, u32[]{:S(2)}, u32[]{:S(2)}) collective-permute-start(bf16[8,2,128,128]{3,2,1,0:T(8,128)(2,1)S(1)} %slice.8), channel_id=1, source_target_pairs={{0,32},{16,48},{32,64},{48,80},{64,96},{80,112},{1,33},{17,49},{33... | collective-permute-start | bytes 1572872 | tf_op jit(solution)/shard_map/ppermute | solution.py:180
  54.3 3.0 %collective-permute-start = (bf16[8,2,128,128]{3,2,1,0:T(8,128)(2,1)S(1)}, bf16[8,2,128,128]{3,2,1,0:T(8,128)(2,1)}, u32[]{:S(2)}, u32[]{:S(2)}) collective-permute-start(bf16[8,2,128,128]{3,2,1,0:T(8,128)(2,1)S(1)} %slice.8), channel_id=1, source_target_pairs={{0,16},{16,32},{32,48},{48,64},{64,80},{80,96},{96,112},{1,17},{17... | collective-permute-start | bytes 1572872 | tf_op jit(solution)/shard_map/ppermute | solution.py:180
  57.3 1.3 fusion
  60.0 0.6 add_convert_fusion.flags_ref
  60.5 58.7 %all-to-all-done.2.x_ref = bf16[16,4,128,128]{3,2,1,0:T(8,128)(2,1)S(1)} async-done(((bf16[16,4,128,128]{3,2,1,0:T(8,128)(2,1)}), bf16[16,4,128,128]{3,2,1,0:T(8,128)(2,1)S(1)}, u32[]{:S(2)}, u32[]{:S(2)}) %all-to-all-start.2) | async-done | bytes 2097184 | tf_op jit(solution)/shard_map/all_to_all | solution.py:184
  119.2 0.0 copy-start.1
  119.2 2.1 collective-permute-start.3
  121.4 2.1 collective-permute-start.2
  123.5 0.0 collective-permute-done.1.far_ref
  123.5 0.0 collective-permute-done.near_ref
  123.5 22.5 %attention.2 = bf16[16,4,128,128]{3,2,1,0:T(8,128)(2,1)} custom-call(s32[2]{0:T(128)} %add_convert_fusion.flags_ref, bf16[16,4,128,128]{3,2,1,0:T(8,128)(2,1)} %all_to_all.20.x_ref, bf16[8,2,128,128]{3,2,1,0:T(8,128)(2,1)} %collective-permute-done.near_ref, bf16[8,2,128,128]{3,2,1,0:T(8,128)(2,1)} %collective-permute-done.1.far_ref), custom_call_target="tpu_custom_call" | custom-call | flops 40000000000 | bytes 6291456 | tf_op jit(solution)/shard_map/attention/pallas_call | solution.py:111
  146.0 0.0 copy-done.1
  146.0 5.0 %all-to-all-start.1 = ((bf16[16,4,128,128]{3,2,1,0:T(8,128)(2,1)}), bf16[16,4,128,128]{3,2,1,0:T(8,128)(2,1)S(1)}, u32[]{:S(2)}, u32[]{:S(2)}) async-start(bf16[16,4,128,128]{3,2,1,0:T(8,128)(2,1)} %attention.2), calls=%async_computation.1 | async-start | bytes 4194304 | tf_op jit(solution)/shard_map/all_to_all | solution.py:184
  151.0 0.0 collective-permute-done.3.far_ref
  151.0 0.0 collective-permute-done.2.near_ref
  151.0 22.7 %attention.3 = bf16[16,4,128,128]{3,2,1,0:T(8,128)(2,1)} custom-call(s32[2]{0:T(128)} %add_convert_fusion.flags_ref, bf16[16,4,128,128]{3,2,1,0:T(8,128)(2,1)} %copy-done.1, bf16[8,2,128,128]{3,2,1,0:T(8,128)(2,1)} %collective-permute-done.2.near_ref, bf16[8,2,128,128]{3,2,1,0:T(8,128)(2,1)} %collective-permute-done.3.far_ref), custom_call_target="tpu_custom_call" | custom-call | flops 40000000000 | bytes 6291456 | tf_op jit(solution)/shard_map/attention/pallas_call | solution.py:111
  173.7 5.7 %all-to-all-done.1.a_ref = bf16[16,4,128,128]{3,2,1,0:T(8,128)(2,1)S(1)} async-done(((bf16[16,4,128,128]{3,2,1,0:T(8,128)(2,1)}), bf16[16,4,128,128]{3,2,1,0:T(8,128)(2,1)S(1)}, u32[]{:S(2)}, u32[]{:S(2)}) %all-to-all-start.1) | async-done | bytes 2097184 | tf_op jit(solution)/shard_map/all_to_all | solution.py:184
  179.4 33.8 %all_to_all.21.b_ref = bf16[16,4,128,128]{3,2,1,0:T(8,128)(2,1)} all-to-all(bf16[16,4,128,128]{3,2,1,0:T(8,128)(2,1)} %attention.3), channel_id=1, replica_groups=mesh['span'=8,'seq'=16] {'seq'}, dimensions={0} | all-to-all | bytes 4194304 | tf_op jit(solution)/shard_map/all_to_all | solution.py:184
  213.2 0.0 copy-done
  213.2 5.0 %unpack.1 = (bf16[128,4096]{1,0:T(8,128)(2,1)}, bf16[128,4096]{1,0:T(8,128)(2,1)}, bf16[128,4096]{1,0:T(8,128)(2,1)}, bf16[128,4096]{1,0:T(8,128)(2,1)}) custom-call(bf16[16,4,128,128]{3,2,1,0:T(8,128)(2,1)} %copy-done, bf16[16,4,128,128]{3,2,1,0:T(8,128)(2,1)} %all_to_all.21.b_ref), custom_call_target="tpu_custom_call" | custom-call | bytes 8388608 | tf_op jit(solution)/shard_map/unpack/pallas_call | solution.py:166
  (2 shorter events, 0.0 us)
Async XLA Ops:
  42.9 76.3 %all-to-all-start.2 = ((bf16[16,4,128,128]{3,2,1,0:T(8,128)(2,1)}), bf16[16,4,128,128]{3,2,1,0:T(8,128)(2,1)S(1)}, u32[]{:S(2)}, u32[]{:S(2)}) async-start(bf16[16,4,128,128]{3,2,1,0:T(8,128)(2,1)} %get-tuple-element.7), calls=%async_computation.2 | async-start | bytes 4194304 | tf_op jit(solution)/shard_map/all_to_all | solution.py:184
  48.8 74.7 %collective-permute-start.1 = (bf16[8,2,128,128]{3,2,1,0:T(8,128)(2,1)S(1)}, bf16[8,2,128,128]{3,2,1,0:T(8,128)(2,1)}, u32[]{:S(2)}, u32[]{:S(2)}) collective-permute-start(bf16[8,2,128,128]{3,2,1,0:T(8,128)(2,1)S(1)} %slice.8), channel_id=1, source_target_pairs={{0,32},{16,48},{32,64},{48,80},{64,96},{80,112},{1,33},{17,49},{33... | collective-permute-start | bytes 1572872 | tf_op jit(solution)/shard_map/ppermute | solution.py:180
  54.3 69.2 %collective-permute-start = (bf16[8,2,128,128]{3,2,1,0:T(8,128)(2,1)S(1)}, bf16[8,2,128,128]{3,2,1,0:T(8,128)(2,1)}, u32[]{:S(2)}, u32[]{:S(2)}) collective-permute-start(bf16[8,2,128,128]{3,2,1,0:T(8,128)(2,1)S(1)} %slice.8), channel_id=1, source_target_pairs={{0,16},{16,32},{32,48},{48,64},{64,80},{80,96},{96,112},{1,17},{17... | collective-permute-start | bytes 1572872 | tf_op jit(solution)/shard_map/ppermute | solution.py:180
  119.2 26.8 %copy-start.1 = (bf16[16,4,128,128]{3,2,1,0:T(8,128)(2,1)}, bf16[16,4,128,128]{3,2,1,0:T(8,128)(2,1)S(1)}, u32[]{:S(2)}) copy-start(bf16[16,4,128,128]{3,2,1,0:T(8,128)(2,1)S(1)} %all-to-all-done.2.x_ref) | copy-start | bytes 6291460
  119.2 31.7 %collective-permute-start.3 = (bf16[8,2,128,128]{3,2,1,0:T(8,128)(2,1)S(1)}, bf16[8,2,128,128]{3,2,1,0:T(8,128)(2,1)}, u32[]{:S(2)}, u32[]{:S(2)}) collective-permute-start(bf16[8,2,128,128]{3,2,1,0:T(8,128)(2,1)S(1)} %slice.9), channel_id=1, source_target_pairs={{0,32},{16,48},{32,64},{48,80},{64,96},{80,112},{1,33},{17,49},{33... | collective-permute-start | bytes 1572872 | tf_op jit(solution)/shard_map/ppermute | solution.py:180
  121.4 29.6 %collective-permute-start.2 = (bf16[8,2,128,128]{3,2,1,0:T(8,128)(2,1)S(1)}, bf16[8,2,128,128]{3,2,1,0:T(8,128)(2,1)}, u32[]{:S(2)}, u32[]{:S(2)}) collective-permute-start(bf16[8,2,128,128]{3,2,1,0:T(8,128)(2,1)S(1)} %slice.9), channel_id=1, source_target_pairs={{0,16},{16,32},{32,48},{48,64},{64,80},{80,96},{96,112},{1,17},{17... | collective-permute-start | bytes 1572872 | tf_op jit(solution)/shard_map/ppermute | solution.py:180
  146.0 33.4 %all-to-all-start.1 = ((bf16[16,4,128,128]{3,2,1,0:T(8,128)(2,1)}), bf16[16,4,128,128]{3,2,1,0:T(8,128)(2,1)S(1)}, u32[]{:S(2)}, u32[]{:S(2)}) async-start(bf16[16,4,128,128]{3,2,1,0:T(8,128)(2,1)} %attention.2), calls=%async_computation.1 | async-start | bytes 4194304 | tf_op jit(solution)/shard_map/all_to_all | solution.py:184
  179.4 33.8 %copy-start = (bf16[16,4,128,128]{3,2,1,0:T(8,128)(2,1)}, bf16[16,4,128,128]{3,2,1,0:T(8,128)(2,1)S(1)}, u32[]{:S(2)}) copy-start(bf16[16,4,128,128]{3,2,1,0:T(8,128)(2,1)S(1)} %all-to-all-done.1.a_ref) | copy-start | bytes 6291460

commit v2 on v1

--- a/solution.py
+++ b/solution.py
@@ -31,13 +31,13 @@
 
 
 def attention_kernel(
-    q_rows, k_cols, flags_ref, x_ref, near_ref, far_ref, out_ref, k_s, v_s, s_s, dp_s, dk_s, dv_s
+    q_rows, k_cols, flags_ref, kv_ref, qg_ref, near_ref, far_ref, out_ref, k_s, v_s, s_s, dp_s, dk_s, dv_s
 ):
-    rows = x_ref.shape[0] * DH
+    rows = qg_ref.shape[0] * DH
     half = near_ref.shape[0] * DH
     near, far = flags_ref[0], flags_ref[1]
-    k_s[:rows] = x_ref[:, 0].reshape(rows, DH)
-    v_s[:rows] = x_ref[:, 1].reshape(rows, DH)
+    k_s[:rows] = kv_ref[:, 0, 0].reshape(rows, DH)
+    v_s[:rows] = kv_ref[:, 0, 1].reshape(rows, DH)
 
     @pl.when(near > 0)
     def _():
@@ -59,8 +59,8 @@
 
         def block(i, carry):
             here = pl.ds(i * group, group)
-            q = x_ref[here, 2].reshape(q_rows, DH)
-            g = x_ref[here, 3].reshape(q_rows, DH)
+            q = qg_ref[here, 0].reshape(q_rows, DH)
+            g = qg_ref[here, 1].reshape(q_rows, DH)
             top = None
             for c in chunks:
                 s = dot(q, k_s[c : c + k_cols], NT)
@@ -104,15 +104,27 @@
     out_ref[:, 3] = dv_s[...].astype(BF16).reshape(rows // DH, DH, DH)
 
 
-def attention(flags, x, near, far, q_rows=256, k_cols=1024):
-    rows, half = x.shape[0] * DH, near.shape[0] * DH
+def attention(flags, unit, kv, qg, near, far, q_rows=256, k_cols=1024):
+    sources = qg.shape[0]
+    rows, half = sources * DH, near.shape[0] * DH
     length = rows + 2 * half
-    vmem = pl.BlockSpec(memory_space=pltpu.VMEM)
+
+    def whole(array):
+        return pl.BlockSpec(array.shape, lambda i: (0,) * array.ndim)
+
+    out = jax.ShapeDtypeStruct((sources, 4, DH, DH), BF16)
     return pl.pallas_call(
         functools.partial(attention_kernel, q_rows, k_cols),
-        out_shape=jax.ShapeDtypeStruct(x.shape, BF16),
-        in_specs=[pl.BlockSpec(memory_space=pltpu.SMEM), vmem, vmem, vmem],
-        out_specs=vmem,
+        grid=(1,),
+        out_shape=out,
+        in_specs=[
+            pl.BlockSpec(memory_space=pltpu.SMEM),
+            pl.BlockSpec((sources, 1, 2, DH, DH), lambda i: (0, unit, 0, 0, 0)),
+            whole(qg),
+            whole(near),
+            whole(far),
+        ],
+        out_specs=whole(out),
         scratch_shapes=[
             pltpu.VMEM((length, DH), BF16),
             pltpu.VMEM((length, DH), BF16),
@@ -126,58 +138,81 @@
             flops=40 * 10**9, bytes_accessed=6 * 2**20, transcendentals=rows * length
         ),
         name="attention",
-    )(flags, x, near, far)
-
-
-def pack_kernel(k_ref, v_ref, q_ref, g_ref, a_ref, b_ref):
+    )(flags, kv, qg, near, far)
+
+
+def column(unit, dest, flip):
+    pair = dest + flip * (2 - dest % 4 // 2 * 4) if dest % 2 else dest
+    return pl.ds(pl.multiple_of((2 * pair + unit) * DH, DH), DH)
+
+
+def pack_kernel(flip_ref, x_ref, y_ref, a_ref, b_ref):
     for j in range(a_ref.shape[0]):
-        for i, ref in enumerate((k_ref, v_ref, q_ref, g_ref)):
-            a_ref[j, i] = ref[:, 2 * j * DH : (2 * j + 1) * DH]
-            b_ref[j, i] = ref[:, (2 * j + 1) * DH : (2 * j + 2) * DH]
-
-
-def pack(arrays):
+        for i, ref in enumerate((x_ref, y_ref)):
+            a_ref[j, i] = ref[:, column(0, j, flip_ref[0])]
+            b_ref[j, i] = ref[:, column(1, j, flip_ref[0])]
+
+
+def pack_joint_kernel(flip_ref, x_ref, y_ref, out_ref):
+    for j in range(out_ref.shape[0]):
+        for i, ref in enumerate((x_ref, y_ref)):
+            for unit in range(2):
+                out_ref[j, unit, i] = ref[:, column(unit, j, flip_ref[0])]
+
+
+def pack(flip, arrays, joint, step=8):
     tokens, width = arrays[0].shape
     dests = width // (2 * DH)
-    step = 4
-    shape = jax.ShapeDtypeStruct((dests, 4, tokens, DH), BF16)
+    if joint:
+        kernel, dims, count = pack_joint_kernel, (2, 2, tokens, DH), 1
+    else:
+        kernel, dims, count = pack_kernel, (2, tokens, DH), 2
+    spec = pl.BlockSpec((step, *dims), lambda j: (j,) + (0,) * len(dims))
+    columns = pl.BlockSpec((tokens, step * 2 * DH), lambda j: (0, j))
     return pl.pallas_call(
-        pack_kernel,
+        kernel,
         grid=(dests // step,),
-        out_shape=(shape, shape),
-        in_specs=[pl.BlockSpec((tokens, step * 2 * DH), lambda j: (0, j))] * 4,
-        out_specs=[pl.BlockSpec((step, 4, tokens, DH), lambda j: (j, 0, 0, 0))] * 2,
-        cost_estimate=pl.CostEstimate(flops=0, bytes_accessed=8 * 2**20, transcendentals=0),
+        out_shape=(jax.ShapeDtypeStruct((dests, *dims), BF16),) * count,
+        in_specs=[pl.BlockSpec(memory_space=pltpu.SMEM), columns, columns],
+        out_specs=[spec] * count,
+        compiler_params=pltpu.CompilerParams(vmem_limit_bytes=VMEM_LIMIT),
+        cost_estimate=pl.CostEstimate(flops=0, bytes_accessed=4 * 2**20, transcendentals=0),
         name="pack",
-    )(*arrays)
-
-
-def unpack_kernel(a_ref, b_ref, *out_refs):
+    )(flip, *arrays)
+
+
+def unpack_kernel(flip_ref, a_ref, b_ref, *out_refs):
     for j in range(a_ref.shape[0]):
         for i, ref in enumerate(out_refs):
-            ref[:, 2 * j * DH : (2 * j + 1) * DH] = a_ref[j, i]
-            ref[:, (2 * j + 1) * DH : (2 * j + 2) * DH] = b_ref[j, i]
-
-
-def unpack(a, b):
+            ref[:, column(0, j, flip_ref[0])] = a_ref[j, i]
+            ref[:, column(1, j, flip_ref[0])] = b_ref[j, i]
+
+
+def unpack(flip, a, b, step=8):
     sources, _, tokens, _ = a.shape
-    step = 4
     shape = jax.ShapeDtypeStruct((tokens, sources * 2 * DH), BF16)
     return pl.pallas_call(
         unpack_kernel,
         grid=(sources // step,),
         out_shape=(shape,) * 4,
-        in_specs=[pl.BlockSpec((step, 4, tokens, DH), lambda j: (j, 0, 0, 0))] * 2,
+        in_specs=[pl.BlockSpec(memory_space=pltpu.SMEM)]
+        + [pl.BlockSpec((step, 4, tokens, DH), lambda j: (j, 0, 0, 0))] * 2,
         out_specs=[pl.BlockSpec((tokens, step * 2 * DH), lambda j: (0, j))] * 4,
+        compiler_params=pltpu.CompilerParams(vmem_limit_bytes=VMEM_LIMIT),
         cost_estimate=pl.CostEstimate(flops=0, bytes_accessed=8 * 2**20, transcendentals=0),
         name="unpack",
-    )(a, b)
-
-
-def passed_along(block, axis, distance):
-    devices = range(lax.axis_size(axis))
-    route = [(i - distance, i) for i in devices if i - distance in devices]
-    return lax.ppermute(block, axis, route)
+    )(flip, a, b)
+
+
+def passed_along(block, distance):
+    spans, width = lax.axis_size("span"), lax.axis_size("seq")
+    route = []
+    for c in range(spans - distance):
+        crosses = (c < spans // 2) != (c + distance < spans // 2)
+        for j in range(width):
+            to = j ^ 2 if crosses and j % 2 else j
+            route.append((c * width + j, (c + distance) * width + to))
+    return lax.ppermute(block, ("span", "seq"), route)
 
 
 def exchange(block):
@@ -189,13 +224,16 @@
     near = jnp.where(span >= 1, block_table[span, jnp.maximum(span - 1, 0)], 0) > 0
     far = jnp.where(span >= 2, block_table[span, jnp.maximum(span - 2, 0)], 0) > 0
     flags = jnp.stack([near, far]).astype(jnp.int32)
+    flip = (span >= lax.axis_size("span") // 2).astype(jnp.int32)[None]
+    kv = exchange(pack(flip, (keys, values), True)[0])
+    packed = pack(flip, (queries, out_grad), False)
+    tails = [kv[kv.shape[0] // 2 :, unit] for unit in range(2)]
+    contexts = [(passed_along(t, 1), passed_along(t, 2)) for t in tails]
     results = []
-    for packed in pack((keys, values, queries, out_grad)):
-        x = exchange(packed)
-        tail = x[x.shape[0] // 2 :, :2]
-        y = attention(flags, x, passed_along(tail, "span", 1), passed_along(tail, "span", 2))
+    for unit in range(2):
+        y = attention(flags, unit, kv, exchange(packed[unit]), *contexts[unit])
         results.append(exchange(y))
-    attended, query_grad, key_grad, value_grad = unpack(*results)
+    attended, query_grad, key_grad, value_grad = unpack(flip, *results)
     return (attended, query_grad, key_grad, value_grad)
 
 

time: 219 us -> 194 us (0.89)
  the two profiles are of different devices: /device:TPU:1 before, /device:TPU:4 now
where the time goes in v2:
time: 194 us; the launch traced here: 192 us
  Pallas kernels  76.6 us (39%)
  starting transfers between devices  40.4 us (21%)
  blocking collectives  36.5 us (19%)
  waiting for transfers between devices  31.6 us (16%)
  local copies, waits for them, and re-layouts  4.43 us (2%)
  between operations  1.94 us (1%)
    pallas_call x2, Pallas kernels, attention(): pl.pallas_call(functools.partial(attention_kernel, q_rows, k_cols), grid=...  67.1 us
    all_to_all x1, blocking collectives, exchange(): return lax.all_to_all(block, 'seq', split_axis=0, concat_axis=0, tiled=True)  36.5 us
    all_to_all x4, starting transfers between devices, exchange(): return lax.all_to_all(block, 'seq', split_axis=0, concat_axis=0, tiled=True)  27.5 us
    all_to_all x4, waiting for transfers between devices, exchange(): return lax.all_to_all(block, 'seq', split_axis=0, concat_axis=0, tiled=True)  27.4 us
    ppermute x4, starting transfers between devices, passed_along(): return lax.ppermute(block, ('span', 'seq'), route)  12.8 us
    pallas_call x2, Pallas kernels, pack(): pl.pallas_call(kernel, grid=(dests // step,), out_shape=(jax.ShapeDtypeSt...  5.47 us
    ppermute x4, waiting for transfers between devices, passed_along(): return lax.ppermute(block, ('span', 'seq'), route)  4.16 us
    pallas_call x1, Pallas kernels, unpack(): pl.pallas_call(unpack_kernel, grid=(sources // step,), out_shape=(shape,)...  4.11 us
  transfers between devices with their start and end apart: 8, of which 4 were waited for; matrix products, arithmetic and copies ran while one was open for 2% of the time, Pallas kernels for 36%

profile of v2, /device:TPU:4, one launch (start us, length us, event | category | flops | bytes accessed | tf_op | source)
XLA Modules:
  0.0 192.0 jit_solution(13000152663314690156)
XLA Ops:
  0.6 2.7 %pack.2 = bf16[16,2,2,128,128]{4,3,2,1,0:T(8,128)(2,1)} custom-call(s32[1]{0:T(128)} %bitcast.flip_ref, bf16[128,4096]{1,0:T(8,128)(2,1)} %x_ref.2, bf16[128,4096]{1,0:T(8,128)(2,1)} %y_ref.2), custom_call_target="tpu_custom_call" | custom-call | bytes 4194304 | tf_op jit(solution)/shard_map/pack/pallas_call | solution.py:172
  3.4 7.9 %all-to-all-start = ((bf16[16,2,2,128,128]{4,3,2,1,0:T(8,128)(2,1)}), bf16[16,2,2,128,128]{4,3,2,1,0:T(8,128)(2,1)S(1)}, u32[]{:S(2)}, u32[]{:S(2)}) async-start(bf16[16,2,2,128,128]{4,3,2,1,0:T(8,128)(2,1)} %pack.2), calls=%async_computation | async-start | bytes 4194304 | tf_op jit(solution)/shard_map/all_to_all | solution.py:219
  11.3 2.7 %pack.3 = (bf16[16,2,128,128]{3,2,1,0:T(8,128)(2,1)}, bf16[16,2,128,128]{3,2,1,0:T(8,128)(2,1)}) custom-call(s32[1]{0:T(128)} %bitcast.flip_ref, bf16[128,4096]{1,0:T(8,128)(2,1)} %x_ref.3, bf16[128,4096]{1,0:T(8,128)(2,1)} %y_ref.3), custom_call_target="tpu_custom_call" | custom-call | bytes 4194304 | tf_op jit(solution)/shard_map/pack/pallas_call | solution.py:172
  14.0 26.5 %all-to-all-done.kv_ref = bf16[16,2,2,128,128]{4,3,2,1,0:T(8,128)(2,1)S(1)} async-done(((bf16[16,2,2,128,128]{4,3,2,1,0:T(8,128)(2,1)}), bf16[16,2,2,128,128]{4,3,2,1,0:T(8,128)(2,1)S(1)}, u32[]{:S(2)}, u32[]{:S(2)}) %all-to-all-start) | async-done | bytes 2097184 | tf_op jit(solution)/shard_map/all_to_all | solution.py:219
  40.5 4.9 %all-to-all-start.3 = ((bf16[16,2,128,128]{3,2,1,0:T(8,128)(2,1)}), bf16[16,2,128,128]{3,2,1,0:T(8,128)(2,1)S(1)}, u32[]{:S(2)}, u32[]{:S(2)}) async-start(bf16[16,2,128,128]{3,2,1,0:T(8,128)(2,1)} %get-tuple-element.7), calls=%async_computation.3 | async-start | bytes 2097152 | tf_op jit(solution)/shard_map/all_to_all | solution.py:219
  45.4 1.0 slice_bitcast_fusion
  46.4 3.1 %collective-permute-start.2 = (bf16[8,2,128,128]{3,2,1,0:T(8,128)(2,1)}, bf16[8,2,128,128]{3,2,1,0:T(8,128)(2,1)S(1)}, u32[]{:S(2)}, u32[]{:S(2)}) collective-permute-start(bf16[8,2,128,128]{3,2,1,0:T(8,128)(2,1)} %get-tuple-element.8), channel_id=1, source_target_pairs={{0,16},{1,17},{2,18},{3,19},{4,20},{5,21},{6,22},{7,23},{8,24},{9,... | collective-permute-start | bytes 1572872 | tf_op jit(solution)/shard_map/ppermute | solution.py:215
  49.5 3.2 %collective-permute-start.3 = (bf16[8,2,128,128]{3,2,1,0:T(8,128)(2,1)}, bf16[8,2,128,128]{3,2,1,0:T(8,128)(2,1)S(1)}, u32[]{:S(2)}, u32[]{:S(2)}) collective-permute-start(bf16[8,2,128,128]{3,2,1,0:T(8,128)(2,1)} %get-tuple-element.8), channel_id=1, source_target_pairs={{0,32},{1,33},{2,34},{3,35},{4,36},{5,37},{6,38},{7,39},{8,40},{9,... | collective-permute-start | bytes 1572872 | tf_op jit(solution)/shard_map/ppermute | solution.py:215
  52.7 1.4 fusion
  55.3 0.6 add_convert_fusion.flags_ref
  55.9 4.0 %collective-permute-start = (bf16[8,2,128,128]{3,2,1,0:T(8,128)(2,1)}, bf16[8,2,128,128]{3,2,1,0:T(8,128)(2,1)}, u32[]{:S(2)}, u32[]{:S(2)}) collective-permute-start(bf16[8,2,128,128]{3,2,1,0:T(8,128)(2,1)} %get-tuple-element.9), channel_id=1, source_target_pairs={{0,16},{1,17},{2,18},{3,19},{4,20},{5,21},{6,22},{7,23},{8,24},{9,... | collective-permute-start | bytes 1572872 | tf_op jit(solution)/shard_map/ppermute | solution.py:215
  59.9 2.6 %collective-permute-start.1 = (bf16[8,2,128,128]{3,2,1,0:T(8,128)(2,1)}, bf16[8,2,128,128]{3,2,1,0:T(8,128)(2,1)}, u32[]{:S(2)}, u32[]{:S(2)}) collective-permute-start(bf16[8,2,128,128]{3,2,1,0:T(8,128)(2,1)} %get-tuple-element.9), channel_id=1, source_target_pairs={{0,32},{1,33},{2,34},{3,35},{4,36},{5,37},{6,38},{7,39},{8,40},{9,... | collective-permute-start | bytes 1572872 | tf_op jit(solution)/shard_map/ppermute | solution.py:215
  62.5 0.9 all-to-all-done.3.qg_ref
  63.4 7.0 %all-to-all-start.1 = ((bf16[16,2,128,128]{3,2,1,0:T(8,128)(2,1)}), bf16[16,2,128,128]{3,2,1,0:T(8,128)(2,1)S(1)}, u32[]{:S(2)}, u32[]{:S(2)}) async-start(bf16[16,2,128,128]{3,2,1,0:T(8,128)(2,1)} %get-tuple-element.6), calls=%async_computation.1 | async-start | bytes 2097152 | tf_op jit(solution)/shard_map/all_to_all | solution.py:219
  70.4 3.6 %collective-permute-done.2.near_ref = bf16[8,2,128,128]{3,2,1,0:T(8,128)(2,1)S(1)} collective-permute-done((bf16[8,2,128,128]{3,2,1,0:T(8,128)(2,1)}, bf16[8,2,128,128]{3,2,1,0:T(8,128)(2,1)S(1)}, u32[]{:S(2)}, u32[]{:S(2)}) %collective-permute-start.2) | collective-permute-done | bytes 524320 | tf_op jit(solution)/shard_map/ppermute | solution.py:215
  73.9 0.6 collective-permute-done.3.far_ref
  74.5 0.2 copy-done.4
  74.7 0.8 copy-done.5
  75.5 33.4 %attention.3 = bf16[16,4,128,128]{3,2,1,0:T(8,128)(2,1)} custom-call(s32[2]{0:T(128)} %add_convert_fusion.flags_ref, bf16[16,2,2,128,128]{4,3,2,1,0:T(8,128)(2,1)} %copy-done.1, bf16[16,2,128,128]{3,2,1,0:T(8,128)(2,1)} %copy-done.2, bf16[8,2,128,128]{3,2,1,0:T(8,128)(2,1)} %copy-done.4, bf16[8,2,128,128]{3,2,1,0:T(8,128)(2,1)} %copy-done.5), custom_call_target="tpu_custom_call" | custom-call | flops 40000000000 | bytes 6291456 | tf_op jit(solution)/shard_map/attention/pallas_call | solution.py:116
  109.0 1.0 copy-done.3
  109.9 7.8 %all-to-all-start.4 = ((bf16[16,4,128,128]{3,2,1,0:T(8,128)(2,1)}), bf16[16,4,128,128]{3,2,1,0:T(8,128)(2,1)S(1)}, u32[]{:S(2)}, u32[]{:S(2)}) async-start(bf16[16,4,128,128]{3,2,1,0:T(8,128)(2,1)} %attention.3), calls=%async_computation.4 | async-start | bytes 4194304 | tf_op jit(solution)/shard_map/all_to_all | solution.py:219
  117.8 33.6 %attention.2 = bf16[16,4,128,128]{3,2,1,0:T(8,128)(2,1)} custom-call(s32[2]{0:T(128)} %add_convert_fusion.flags_ref, bf16[16,2,2,128,128]{4,3,2,1,0:T(8,128)(2,1)} %copy-done.1, bf16[16,2,128,128]{3,2,1,0:T(8,128)(2,1)} %copy-done.3, bf16[8,2,128,128]{3,2,1,0:T(8,128)(2,1)} %collective-permute-done.near_ref, ...), custom_call_target="tpu_custom_call" | custom-call | flops 40000000000 | bytes 6291456 | tf_op jit(solution)/shard_map/attention/pallas_call | solution.py:116
  151.4 36.5 %all_to_all.25.a_ref = bf16[16,4,128,128]{3,2,1,0:T(8,128)(2,1)} all-to-all(bf16[16,4,128,128]{3,2,1,0:T(8,128)(2,1)} %attention.2), channel_id=1, replica_groups=mesh['span'=8,'seq'=16] {'seq'}, dimensions={0} | all-to-all | bytes 4194304 | tf_op jit(solution)/shard_map/all_to_all | solution.py:219
  187.9 4.1 %unpack.1 = (bf16[128,4096]{1,0:T(8,128)(2,1)}, bf16[128,4096]{1,0:T(8,128)(2,1)}, bf16[128,4096]{1,0:T(8,128)(2,1)}, bf16[128,4096]{1,0:T(8,128)(2,1)}) custom-call(s32[1]{0:T(128)} %bitcast.flip_ref, bf16[16,4,128,128]{3,2,1,0:T(8,128)(2,1)} %all_to_all.25.a_ref, bf16[16,4,128,128]{3,2,1,0:T(8,128)(2,1)} %copy-done), custom_call_target="tpu_custom_call" | custom-call | bytes 8388608 | tf_op jit(solution)/shard_map/unpack/pallas_call | solution.py:194
  (13 shorter events, 0.0 us)
Async XLA Ops:
  3.4 37.1 %all-to-all-start = ((bf16[16,2,2,128,128]{4,3,2,1,0:T(8,128)(2,1)}), bf16[16,2,2,128,128]{4,3,2,1,0:T(8,128)(2,1)S(1)}, u32[]{:S(2)}, u32[]{:S(2)}) async-start(bf16[16,2,2,128,128]{4,3,2,1,0:T(8,128)(2,1)} %pack.2), calls=%async_computation | async-start | bytes 4194304 | tf_op jit(solution)/shard_map/all_to_all | solution.py:219
  40.5 5.9 %copy-start.1 = (bf16[16,2,2,128,128]{4,3,2,1,0:T(8,128)(2,1)}, bf16[16,2,2,128,128]{4,3,2,1,0:T(8,128)(2,1)S(1)}, u32[]{:S(2)}) copy-start(bf16[16,2,2,128,128]{4,3,2,1,0:T(8,128)(2,1)S(1)} %all-to-all-done.kv_ref) | copy-start | bytes 6291460
  40.5 22.9 %all-to-all-start.3 = ((bf16[16,2,128,128]{3,2,1,0:T(8,128)(2,1)}), bf16[16,2,128,128]{3,2,1,0:T(8,128)(2,1)S(1)}, u32[]{:S(2)}, u32[]{:S(2)}) async-start(bf16[16,2,128,128]{3,2,1,0:T(8,128)(2,1)} %get-tuple-element.7), calls=%async_computation.3 | async-start | bytes 2097152 | tf_op jit(solution)/shard_map/all_to_all | solution.py:219
  46.4 27.5 %collective-permute-start.2 = (bf16[8,2,128,128]{3,2,1,0:T(8,128)(2,1)}, bf16[8,2,128,128]{3,2,1,0:T(8,128)(2,1)S(1)}, u32[]{:S(2)}, u32[]{:S(2)}) collective-permute-start(bf16[8,2,128,128]{3,2,1,0:T(8,128)(2,1)} %get-tuple-element.8), channel_id=1, source_target_pairs={{0,16},{1,17},{2,18},{3,19},{4,20},{5,21},{6,22},{7,23},{8,24},{9,... | collective-permute-start | bytes 1572872 | tf_op jit(solution)/shard_map/ppermute | solution.py:215
  49.5 25.0 %collective-permute-start.3 = (bf16[8,2,128,128]{3,2,1,0:T(8,128)(2,1)}, bf16[8,2,128,128]{3,2,1,0:T(8,128)(2,1)S(1)}, u32[]{:S(2)}, u32[]{:S(2)}) collective-permute-start(bf16[8,2,128,128]{3,2,1,0:T(8,128)(2,1)} %get-tuple-element.8), channel_id=1, source_target_pairs={{0,32},{1,33},{2,34},{3,35},{4,36},{5,37},{6,38},{7,39},{8,40},{9,... | collective-permute-start | bytes 1572872 | tf_op jit(solution)/shard_map/ppermute | solution.py:215
  55.9 61.8 %collective-permute-start = (bf16[8,2,128,128]{3,2,1,0:T(8,128)(2,1)}, bf16[8,2,128,128]{3,2,1,0:T(8,128)(2,1)}, u32[]{:S(2)}, u32[]{:S(2)}) collective-permute-start(bf16[8,2,128,128]{3,2,1,0:T(8,128)(2,1)} %get-tuple-element.9), channel_id=1, source_target_pairs={{0,16},{1,17},{2,18},{3,19},{4,20},{5,21},{6,22},{7,23},{8,24},{9,... | collective-permute-start | bytes 1572872 | tf_op jit(solution)/shard_map/ppermute | solution.py:215
  59.9 57.8 %collective-permute-start.1 = (bf16[8,2,128,128]{3,2,1,0:T(8,128)(2,1)}, bf16[8,2,128,128]{3,2,1,0:T(8,128)(2,1)}, u32[]{:S(2)}, u32[]{:S(2)}) collective-permute-start(bf16[8,2,128,128]{3,2,1,0:T(8,128)(2,1)} %get-tuple-element.9), channel_id=1, source_target_pairs={{0,32},{1,33},{2,34},{3,35},{4,36},{5,37},{6,38},{7,39},{8,40},{9,... | collective-permute-start | bytes 1572872 | tf_op jit(solution)/shard_map/ppermute | solution.py:215
  63.4 11.1 %copy-start.2 = (bf16[16,2,128,128]{3,2,1,0:T(8,128)(2,1)}, bf16[16,2,128,128]{3,2,1,0:T(8,128)(2,1)S(1)}, u32[]{:S(2)}) copy-start(bf16[16,2,128,128]{3,2,1,0:T(8,128)(2,1)S(1)} %all-to-all-done.3.qg_ref) | copy-start | bytes 3145732
  63.4 45.6 %all-to-all-start.1 = ((bf16[16,2,128,128]{3,2,1,0:T(8,128)(2,1)}), bf16[16,2,128,128]{3,2,1,0:T(8,128)(2,1)S(1)}, u32[]{:S(2)}, u32[]{:S(2)}) async-start(bf16[16,2,128,128]{3,2,1,0:T(8,128)(2,1)} %get-tuple-element.6), calls=%async_computation.1 | async-start | bytes 2097152 | tf_op jit(solution)/shard_map/all_to_all | solution.py:219
  73.9 0.8 copy-start.4
  74.7 0.8 copy-start.5
  109.0 1.0 copy-start.3
  109.9 41.5 %all-to-all-start.4 = ((bf16[16,4,128,128]{3,2,1,0:T(8,128)(2,1)}), bf16[16,4,128,128]{3,2,1,0:T(8,128)(2,1)S(1)}, u32[]{:S(2)}, u32[]{:S(2)}) async-start(bf16[16,4,128,128]{3,2,1,0:T(8,128)(2,1)} %attention.3), calls=%async_computation.4 | async-start | bytes 4194304 | tf_op jit(solution)/shard_map/all_to_all | solution.py:219
  151.4 36.5 %copy-start = (bf16[16,4,128,128]{3,2,1,0:T(8,128)(2,1)}, bf16[16,4,128,128]{3,2,1,0:T(8,128)(2,1)S(1)}, u32[]{:S(2)}) copy-start(bf16[16,4,128,128]{3,2,1,0:T(8,128)(2,1)S(1)} %all-to-all-done.4.b_ref) | copy-start | bytes 6291460

commit v3 on v2

v3 whole, which is shorter than its diff:
```python
import functools
import math

import jax
import jax.numpy as jnp
from jax import lax
from jax.experimental import pallas as pl
from jax.experimental.pallas import tpu as pltpu
from jax.sharding import PartitionSpec as P

DH = 128
F32 = jnp.float32
BF16 = jnp.bfloat16
SCALE = 1.0 / math.sqrt(DH)
SCALE2 = SCALE * math.log2(math.e)
NT = (((1,), (1,)), ((), ()))
NN = (((1,), (0,)), ((), ()))
TN = (((0,), (0,)), ((), ()))
ATTENTION_VMEM = 50 * 2**20
COPY_VMEM = 16 * 2**20


def dot(a, b, dims):
    return lax.dot_general(a, b, dims, preferred_element_type=F32)


def fold(op, x):
    result = x[:, :DH]
    for i in range(DH, x.shape[1], DH):
        result = op(result, x[:, i : i + DH])
    return result


def attention_kernel(
    q_rows, k_cols, unit, flags_ref, kv_ref, qg_hbm, far_ref, near_ref, out_ref,
    k_s, v_s, qg_ref, s_s, dp_s, dk_s, dv_s, sems
):
    sources, half = qg_ref.shape[0], near_ref.shape[0]
    rows = sources * DH
    copies = [pltpu.make_async_copy(qg_hbm, qg_ref, sems.at[0])]
    for kind, scratch in enumerate((k_s, v_s)):
        places = (
            (kv_ref.at[:, unit, kind], scratch.at[:sources]),
            (near_ref.at[:, kind], scratch.at[sources : sources + half]),
            (far_ref.at[:, kind], scratch.at[sources + half : sources + 2 * half]),
        )
        for i, (src, dst) in enumerate(places):
            copies.append(pltpu.make_async_copy(src, dst, sems.at[1 + 3 * kind + i]))
    for copy in copies:
        copy.start()
    dk_s[...] = jnp.zeros_like(dk_s)
    dv_s[...] = jnp.zeros_like(dv_s)
    for copy in copies:
        copy.wait()
    group, span = q_rows // DH, k_cols // DH

    def run(near, far):
        parts = list(range(0, sources, span))
        if near:
            parts += range(sources, sources + half, span)
        if far:
            parts += range(sources + half, sources + 2 * half, span)
        chunks = range(0, len(parts) * k_cols, k_cols)

        def part_of(scratch, c):
            i = parts[c // k_cols]
            return scratch[i : i + span].reshape(k_cols, DH)

        def block(i, carry):
            here = pl.ds(i * group, group)
            q = qg_ref[here, 0].reshape(q_rows, DH)
            g = qg_ref[here, 1].reshape(q_rows, DH)
            top = None
            for c in chunks:
                s = dot(q, part_of(k_s, c), NT)
                s_s[:, c : c + k_cols] = s
                part = fold(jnp.maximum, s)
                top = part if top is None else jnp.maximum(top, part)
            top = jnp.max(top, 1, keepdims=True) * SCALE2
            total = delta = out = None
            for c in chunks:
                e = jnp.exp2(s_s[:, c : c + k_cols] * SCALE2 - top)
                s_s[:, c : c + k_cols] = e
                dp = dot(g, part_of(v_s, c), NT)
                dp_s[:, c : c + k_cols] = dp
                t_part, d_part = fold(jnp.add, e), fold(jnp.add, e * dp)
                o_part = dot(e.astype(BF16), part_of(v_s, c), NN)
                total = t_part if total is None else total + t_part
                delta = d_part if delta is None else delta + d_part
                out = o_part if out is None else out + o_part
            inv = 1.0 / jnp.sum(total, 1, keepdims=True)
            delta = jnp.sum(delta, 1, keepdims=True) * inv
            out_ref[here, 0] = (out * inv).astype(BF16).reshape(group, DH, DH)
            g_over = (g.astype(F32) * inv).astype(BF16)
            q_over = (q.astype(F32) * (inv * SCALE)).astype(BF16)
            dq = None
            for c in chunks:
                e = s_s[:, c : c + k_cols]
                ds = (e * (dp_s[:, c : c + k_cols] - delta)).astype(BF16)
                part = dot(ds, part_of(k_s, c), NN)
                dq = part if dq is None else dq + part
                if c < rows:
                    dk_s[c : c + k_cols] += dot(ds, q_over, TN)
                    dv_s[c : c + k_cols] += dot(e.astype(BF16), g_over, TN)
            out_ref[here, 1] = (dq * (inv * SCALE)).astype(BF16).reshape(group, DH, DH)
            return carry

        lax.fori_loop(0, rows // q_rows, block, 0)

    for near in range(2):
        for far in range(2):
            here = (flags_ref[0] == near) & (flags_ref[1] == far)
            pl.when(here)(functools.partial(run, near, far))
    out_ref[:, 2] = dk_s[...].astype(BF16).reshape(rows // DH, DH, DH)
    out_ref[:, 3] = dv_s[...].astype(BF16).reshape(rows // DH, DH, DH)


def attention(flags, unit, kv, qg, near, far, q_rows=256, k_cols=1024):
    sources = qg.shape[0]
    rows, half = sources * DH, near.shape[0] * DH
    length = rows + 2 * half

    hbm = pl.BlockSpec(memory_space=pl.ANY)
    out = jax.ShapeDtypeStruct((sources, 4, DH, DH), BF16)
    return pl.pallas_call(
        functools.partial(attention_kernel, q_rows, k_cols, unit),
        grid=(1,),
        out_shape=out,
        in_specs=[pl.BlockSpec(memory_space=pltpu.SMEM), hbm, hbm, hbm, hbm],
        out_specs=pl.BlockSpec(out.shape, lambda i: (0, 0, 0, 0)),
        scratch_shapes=[
            pltpu.VMEM((length // DH, DH, DH), BF16),
            pltpu.VMEM((length // DH, DH, DH), BF16),
            pltpu.VMEM(qg.shape, BF16),
            pltpu.VMEM((q_rows, length), F32),
            pltpu.VMEM((q_rows, length), F32),
            pltpu.VMEM((rows, DH), F32),
            pltpu.VMEM((rows, DH), F32),
            pltpu.SemaphoreType.DMA((7,)),
        ],
        compiler_params=pltpu.CompilerParams(vmem_limit_bytes=ATTENTION_VMEM),
        cost_estimate=pl.CostEstimate(
            flops=40 * 10**9, bytes_accessed=6 * 2**20, transcendentals=rows * length
        ),
        name="attention",
    )(flags, kv, qg, far, near)


def column(dest, flip):
    head = dest + flip * (2 - dest % 4 // 2 * 4) if dest % 2 else dest
    return pl.ds(pl.multiple_of(head * DH, DH), DH)


def pack_kernel(count, flip_ref, *refs):
    for out_ref, pair in zip(refs[-count:], (refs[:2], refs[2:4])[:count]):
        for j in range(out_ref.shape[0]):
            for i, ref in enumerate(pair):
                out_ref[j, i] = ref[:, column(j, flip_ref[0])]


def pack_joint_kernel(flip_ref, x0_ref, y0_ref, x1_ref, y1_ref, out_ref):
    for unit, pair in enumerate(((x0_ref, y0_ref), (x1_ref, y1_ref))):
        for j in range(out_ref.shape[0]):
            for i, ref in enumerate(pair):
                out_ref[j, unit, i] = ref[:, column(j, flip_ref[0])]


def pack(flip, arrays, joint, step=8):
    tokens, width = arrays[0].shape
    dests = width // (2 * DH)
    steps = dests // step
    if joint:
        kernel, dims, count = pack_joint_kernel, (2, 2, tokens, DH), 1
    else:
        kernel, dims, count = functools.partial(pack_kernel, 2), (2, tokens, DH), 2
    spec = pl.BlockSpec((step, *dims), lambda j: (j,) + (0,) * len(dims))
    left = pl.BlockSpec((tokens, step * DH), lambda j: (0, j))
    right = pl.BlockSpec((tokens, step * DH), lambda j: (0, j + steps))
    return pl.pallas_call(
        kernel,
        grid=(steps,),
        out_shape=(jax.ShapeDtypeStruct((dests, *dims), BF16),) * count,
        in_specs=[pl.BlockSpec(memory_space=pltpu.SMEM), left, left, right, right],
        out_specs=[spec] * count,
        compiler_params=pltpu.CompilerParams(vmem_limit_bytes=56 * 2**20),
        cost_estimate=pl.CostEstimate(flops=0, bytes_accessed=4 * 2**20, transcendentals=0),
        name="pack",
    )(flip, *arrays, *arrays)


def unpack_kernel(step, flip_ref, x_ref, *refs):
    out_refs, (buf, sems) = refs[-6:-2], refs[-2:]
    i = pl.program_id(0)

    def fetch(n):
        return pltpu.make_async_copy(x_ref.at[pl.ds(n * step, step)], buf.at[n], sems.at[n])

    @pl.when(i == 0)
    def _():
        for n in range(buf.shape[0]):
            fetch(n).start()

    fetch(i).wait()
    for j in range(step):
        for kind, ref in enumerate(out_refs):
            ref[:, column(j, flip_ref[0])] = buf[i, j, kind]


def unpack(flip, unit, x, into=(), step=8):
    sources, _, tokens, _ = x.shape
    steps = sources // step
    shape = jax.ShapeDtypeStruct((tokens, sources * 2 * DH), BF16)
    return pl.pallas_call(
        functools.partial(unpack_kernel, step),
        grid=(steps,),
        out_shape=(shape,) * 4,
        in_specs=[
            pl.BlockSpec(memory_space=pltpu.SMEM),
            pl.BlockSpec(memory_space=pl.ANY),
        ]
        + [pl.BlockSpec(memory_space=pl.ANY)] * len(into),
        out_specs=[pl.BlockSpec((tokens, step * DH), lambda j: (0, j + unit * steps))] * 4,
        scratch_shapes=[
            pltpu.VMEM((steps, step, *x.shape[1:]), BF16),
            pltpu.SemaphoreType.DMA((steps,)),
        ],
        input_output_aliases={2 + i: i for i in range(len(into))},
        compiler_params=pltpu.CompilerParams(vmem_limit_bytes=COPY_VMEM),
        cost_estimate=pl.CostEstimate(flops=0, bytes_accessed=4 * 2**20, transcendentals=0),
        name="unpack",
    )(flip, x, *into)


def passed_along(block, distance):
    spans, width = lax.axis_size("span"), lax.axis_size("seq")
    route = []
    for c in range(spans - distance):
        crosses = (c < spans // 2) != (c + distance < spans // 2)
        for j in range(width):
            to = j ^ 2 if crosses and j % 2 else j
            route.append((c * width + j, (c + distance) * width + to))
    return lax.ppermute(block, ("span", "seq"), route)


def exchange(block):
    return lax.all_to_all(block, "seq", split_axis=0, concat_axis=0, tiled=True)


def body(queries, keys, values, out_grad, block_table):
    span = lax.axis_index("span")
    near = jnp.where(span >= 1, block_table[span, jnp.maximum(span - 1, 0)], 0) > 0
    far = jnp.where(span >= 2, block_table[span, jnp.maximum(span - 2, 0)], 0) > 0
    flags = jnp.stack([near, far]).astype(jnp.int32)
    flip = (span >= lax.axis_size("span") // 2).astype(jnp.int32)[None]
    kv = exchange(pack(flip, (keys, values), True)[0])
    packed = pack(flip, (queries, out_grad), False)
    tails = [kv[kv.shape[0] // 2 :, unit] for unit in range(2)]
    contexts = [(passed_along(t, 1), passed_along(t, 2)) for t in tails]
    results = ()
    for unit in range(2):
        y = attention(flags, unit, kv, exchange(packed[unit]), *contexts[unit])
        results = unpack(flip, unit, exchange(y), results)
    return tuple(results)


def solution(mesh):
    rows = P(("span", "seq"), None)
    return jax.shard_map(
        body,
        mesh=mesh,
        in_specs=(rows, rows, rows, rows, P()),
        out_specs=(rows, rows, rows, rows),
        check_vma=False,
    )
```

time: 194 us -> 188 us (0.969)
  the two profiles are of different devices: /device:TPU:4 before, /device:TPU:99 now
where the time goes in v3:
time: 188 us; the launch traced here: 186 us
  Pallas kernels  75.7 us (40%)
  waiting for transfers between devices  55.3 us (29%)
  starting transfers between devices  47.5 us (25%)
  local copies, waits for them, and re-layouts  5.38 us (3%)
  between operations  2.13 us (1%)
    pallas_call x2, Pallas kernels, attention(): pl.pallas_call(functools.partial(attention_kernel, q_rows, k_cols, unit),...  66.8 us
    all_to_all x5, waiting for transfers between devices, exchange(): return lax.all_to_all(block, 'seq', split_axis=0, concat_axis=0, tiled=True)  54.6 us
    all_to_all x5, starting transfers between devices, exchange(): return lax.all_to_all(block, 'seq', split_axis=0, concat_axis=0, tiled=True)  38.4 us
    ppermute x4, starting transfers between devices, passed_along(): return lax.ppermute(block, ('span', 'seq'), route)  9.14 us
    pallas_call x2, Pallas kernels, pack(): pl.pallas_call(kernel, grid=(steps,), out_shape=(jax.ShapeDtypeStruct((de...  5.44 us
  transfers between devices with their start and end apart: 9, of which 4 were waited for; matrix products, arithmetic and copies ran while one was open for 1% of the time, Pallas kernels for 38%

profile of v3, /device:TPU:99, one launch (start us, length us, event | category | flops | bytes accessed | tf_op | source)
XLA Modules:
  0.0 186.2 jit_solution(4364707515697894869)
XLA Ops:
  0.6 2.7 %pack.2 = bf16[16,2,2,128,128]{4,3,2,1,0:T(8,128)(2,1)} custom-call(s32[1]{0:T(128)} %bitcast.flip_ref, bf16[128,4096]{1,0:T(8,128)(2,1)} %x1_ref.1, bf16[128,4096]{1,0:T(8,128)(2,1)} %y1_ref.1, bf16[128,4096]{1,0:T(8,128)(2,1)} %x1_ref.1, bf16[128,4096]{1,0:T(8,128)(2,1)} %y1_ref.1), custom_call_target="tpu_custom_call" | custom-call | bytes 4194304 | tf_op jit(solution)/shard_map/pack/pallas_call | solution.py:179
  3.4 7.8 %all-to-all-start = ((bf16[16,2,2,128,128]{4,3,2,1,0:T(8,128)(2,1)}), bf16[16,2,2,128,128]{4,3,2,1,0:T(8,128)(2,1)S(1)}, u32[]{:S(2)}, u32[]{:S(2)}) async-start(bf16[16,2,2,128,128]{4,3,2,1,0:T(8,128)(2,1)} %pack.2), calls=%async_computation | async-start | bytes 4194304 | tf_op jit(solution)/shard_map/all_to_all | solution.py:246
  11.1 2.7 %pack.3 = (bf16[16,2,128,128]{3,2,1,0:T(8,128)(2,1)}, bf16[16,2,128,128]{3,2,1,0:T(8,128)(2,1)}) custom-call(s32[1]{0:T(128)} %bitcast.flip_ref, bf16[128,4096]{1,0:T(8,128)(2,1)} %refs_2_.1, bf16[128,4096]{1,0:T(8,128)(2,1)} %refs_3_.1, bf16[128,4096]{1,0:T(8,128)(2,1)} %refs_2_.1, bf16[128,4096]{1,0:T(8,128)(2,1)} %refs_3_.1), custom_call_target="tpu_custom_call" | custom-call | bytes 4194304 | tf_op jit(solution)/shard_map/pack/pallas_call | solution.py:179
  13.8 25.9 %all-to-all-done.kv_ref = bf16[16,2,2,128,128]{4,3,2,1,0:T(8,128)(2,1)S(1)} async-done(((bf16[16,2,2,128,128]{4,3,2,1,0:T(8,128)(2,1)}), bf16[16,2,2,128,128]{4,3,2,1,0:T(8,128)(2,1)S(1)}, u32[]{:S(2)}, u32[]{:S(2)}) %all-to-all-start) | async-done | bytes 2097184 | tf_op jit(solution)/shard_map/all_to_all | solution.py:246
  39.8 5.5 %all-to-all-start.3 = ((bf16[16,2,128,128]{3,2,1,0:T(8,128)(2,1)}), bf16[16,2,128,128]{3,2,1,0:T(8,128)(2,1)S(1)}, u32[]{:S(2)}, u32[]{:S(2)}) async-start(bf16[16,2,128,128]{3,2,1,0:T(8,128)(2,1)} %get-tuple-element.11), calls=%async_computation.3 | async-start | bytes 2097152 | tf_op jit(solution)/shard_map/all_to_all | solution.py:246
  45.3 1.0 slice_bitcast_fusion
  46.3 3.1 %collective-permute-start.3 = (bf16[8,2,128,128]{3,2,1,0:T(8,128)(2,1)}, bf16[8,2,128,128]{3,2,1,0:T(8,128)(2,1)S(1)}, u32[]{:S(2)}, u32[]{:S(2)}) collective-permute-start(bf16[8,2,128,128]{3,2,1,0:T(8,128)(2,1)} %get-tuple-element.16), channel_id=1, source_target_pairs={{0,16},{1,17},{2,18},{3,19},{4,20},{5,21},{6,22},{7,23},{8,24},{9,... | collective-permute-start | bytes 1572872 | tf_op jit(solution)/shard_map/ppermute | solution.py:242
  49.4 1.9 %collective-permute-start.2 = (bf16[8,2,128,128]{3,2,1,0:T(8,128)(2,1)}, bf16[8,2,128,128]{3,2,1,0:T(8,128)(2,1)S(1)}, u32[]{:S(2)}, u32[]{:S(2)}) collective-permute-start(bf16[8,2,128,128]{3,2,1,0:T(8,128)(2,1)} %get-tuple-element.16), channel_id=1, source_target_pairs={{0,32},{1,33},{2,34},{3,35},{4,36},{5,37},{6,38},{7,39},{8,40},{9,... | collective-permute-start | bytes 1572872 | tf_op jit(solution)/shard_map/ppermute | solution.py:242
  51.4 1.4 fusion
  54.0 0.1 add_convert_fusion.flags_ref
  54.0 2.2 %collective-permute-start.1 = (bf16[8,2,128,128]{3,2,1,0:T(8,128)(2,1)}, bf16[8,2,128,128]{3,2,1,0:T(8,128)(2,1)}, u32[]{:S(2)}, u32[]{:S(2)}) collective-permute-start(bf16[8,2,128,128]{3,2,1,0:T(8,128)(2,1)} %get-tuple-element.17), channel_id=1, source_target_pairs={{0,16},{1,17},{2,18},{3,19},{4,20},{5,21},{6,22},{7,23},{8,24},{9,... | collective-permute-start | bytes 1572872 | tf_op jit(solution)/shard_map/ppermute | solution.py:242
  56.2 1.9 %collective-permute-start = (bf16[8,2,128,128]{3,2,1,0:T(8,128)(2,1)}, bf16[8,2,128,128]{3,2,1,0:T(8,128)(2,1)}, u32[]{:S(2)}, u32[]{:S(2)}) collective-permute-start(bf16[8,2,128,128]{3,2,1,0:T(8,128)(2,1)} %get-tuple-element.17), channel_id=1, source_target_pairs={{0,32},{1,33},{2,34},{3,35},{4,36},{5,37},{6,38},{7,39},{8,40},{9,... | collective-permute-start | bytes 1572872 | tf_op jit(solution)/shard_map/ppermute | solution.py:242
  58.2 3.4 %all-to-all-done.3.qg_hbm = bf16[16,2,128,128]{3,2,1,0:T(8,128)(2,1)S(1)} async-done(((bf16[16,2,128,128]{3,2,1,0:T(8,128)(2,1)}), bf16[16,2,128,128]{3,2,1,0:T(8,128)(2,1)S(1)}, u32[]{:S(2)}, u32[]{:S(2)}) %all-to-all-start.3) | async-done | bytes 1048608 | tf_op jit(solution)/shard_map/all_to_all | solution.py:246
  61.5 8.1 %all-to-all-start.1 = ((bf16[16,2,128,128]{3,2,1,0:T(8,128)(2,1)}), bf16[16,2,128,128]{3,2,1,0:T(8,128)(2,1)S(1)}, u32[]{:S(2)}, u32[]{:S(2)}) async-start(bf16[16,2,128,128]{3,2,1,0:T(8,128)(2,1)} %get-tuple-element.10), calls=%async_computation.1 | async-start | bytes 2097152 | tf_op jit(solution)/shard_map/all_to_all | solution.py:246
  69.7 0.8 collective-permute-done.2.far_ref
  70.5 33.3 %attention.3 = bf16[16,4,128,128]{3,2,1,0:T(8,128)(2,1)} custom-call(s32[2]{0:T(128)S(1)} %add_convert_fusion.flags_ref, bf16[16,2,2,128,128]{4,3,2,1,0:T(8,128)(2,1)} %copy-done.2, bf16[16,2,128,128]{3,2,1,0:T(8,128)(2,1)S(1)} %all-to-all-done.3.qg_hbm, bf16[8,2,128,128]{3,2,1,0:T(8,128)(2,1)S(1)} %collective-permute-done.2.far_ref, ...), custom_call_target="tpu_custom_call" | custom-call | flops 40000000000 | bytes 6291456 | tf_op jit(solution)/shard_map/attention/pallas_call | solution.py:125
  103.7 9.8 %all-to-all-start.4 = ((bf16[16,4,128,128]{3,2,1,0:T(8,128)(2,1)}), bf16[16,4,128,128]{3,2,1,0:T(8,128)(2,1)S(1)}, u32[]{:S(2)}, u32[]{:S(2)}) async-start(bf16[16,4,128,128]{3,2,1,0:T(8,128)(2,1)} %attention.3), calls=%async_computation.4 | async-start | bytes 4194304 | tf_op jit(solution)/shard_map/all_to_all | solution.py:246
  113.5 33.5 %attention.2 = bf16[16,4,128,128]{3,2,1,0:T(8,128)(2,1)} custom-call(s32[2]{0:T(128)S(1)} %add_convert_fusion.flags_ref, bf16[16,2,2,128,128]{4,3,2,1,0:T(8,128)(2,1)} %copy-done.2, bf16[16,2,128,128]{3,2,1,0:T(8,128)(2,1)S(1)} %all-to-all-done.1.qg_hbm, bf16[8,2,128,128]{3,2,1,0:T(8,128)(2,1)} %collective-permute-done.far_ref, ...), custom_call_target="tpu_custom_call" | custom-call | flops 40000000000 | bytes 6291456 | tf_op jit(solution)/shard_map/attention/pallas_call | solution.py:125
  147.1 1.3 copy-done
  148.4 7.2 %all-to-all-start.2 = ((bf16[16,4,128,128]{3,2,1,0:T(8,128)(2,1)}), bf16[16,4,128,128]{3,2,1,0:T(8,128)(2,1)S(1)}, u32[]{:S(2)}, u32[]{:S(2)}) async-start(bf16[16,4,128,128]{3,2,1,0:T(8,128)(2,1)} %attention.2), calls=%async_computation.2 | async-start | bytes 4194304 | tf_op jit(solution)/shard_map/all_to_all | solution.py:246
  155.6 1.6 copy-done.1
  157.2 1.8 unpack.2
  159.0 25.3 %all-to-all-done.2.x_ref = bf16[16,4,128,128]{3,2,1,0:T(8,128)(2,1)S(1)} async-done(((bf16[16,4,128,128]{3,2,1,0:T(8,128)(2,1)}), bf16[16,4,128,128]{3,2,1,0:T(8,128)(2,1)S(1)}, u32[]{:S(2)}, u32[]{:S(2)}) %all-to-all-start.2) | async-done | bytes 2097184 | tf_op jit(solution)/shard_map/all_to_all | solution.py:246
  184.2 1.8 unpack.3
  (9 shorter events, 0.0 us)
Async XLA Ops:
  3.4 36.4 %all-to-all-start = ((bf16[16,2,2,128,128]{4,3,2,1,0:T(8,128)(2,1)}), bf16[16,2,2,128,128]{4,3,2,1,0:T(8,128)(2,1)S(1)}, u32[]{:S(2)}, u32[]{:S(2)}) async-start(bf16[16,2,2,128,128]{4,3,2,1,0:T(8,128)(2,1)} %pack.2), calls=%async_computation | async-start | bytes 4194304 | tf_op jit(solution)/shard_map/all_to_all | solution.py:246
  39.8 6.5 %copy-start.2 = (bf16[16,2,2,128,128]{4,3,2,1,0:T(8,128)(2,1)}, bf16[16,2,2,128,128]{4,3,2,1,0:T(8,128)(2,1)S(1)}, u32[]{:S(2)}) copy-start(bf16[16,2,2,128,128]{4,3,2,1,0:T(8,128)(2,1)S(1)} %all-to-all-done.kv_ref) | copy-start | bytes 6291460
  39.8 21.8 %all-to-all-start.3 = ((bf16[16,2,128,128]{3,2,1,0:T(8,128)(2,1)}), bf16[16,2,128,128]{3,2,1,0:T(8,128)(2,1)S(1)}, u32[]{:S(2)}, u32[]{:S(2)}) async-start(bf16[16,2,128,128]{3,2,1,0:T(8,128)(2,1)} %get-tuple-element.11), calls=%async_computation.3 | async-start | bytes 2097152 | tf_op jit(solution)/shard_map/all_to_all | solution.py:246
  46.3 23.4 %collective-permute-start.3 = (bf16[8,2,128,128]{3,2,1,0:T(8,128)(2,1)}, bf16[8,2,128,128]{3,2,1,0:T(8,128)(2,1)S(1)}, u32[]{:S(2)}, u32[]{:S(2)}) collective-permute-start(bf16[8,2,128,128]{3,2,1,0:T(8,128)(2,1)} %get-tuple-element.16), channel_id=1, source_target_pairs={{0,16},{1,17},{2,18},{3,19},{4,20},{5,21},{6,22},{7,23},{8,24},{9,... | collective-permute-start | bytes 1572872 | tf_op jit(solution)/shard_map/ppermute | solution.py:242
  49.4 21.0 %collective-permute-start.2 = (bf16[8,2,128,128]{3,2,1,0:T(8,128)(2,1)}, bf16[8,2,128,128]{3,2,1,0:T(8,128)(2,1)S(1)}, u32[]{:S(2)}, u32[]{:S(2)}) collective-permute-start(bf16[8,2,128,128]{3,2,1,0:T(8,128)(2,1)} %get-tuple-element.16), channel_id=1, source_target_pairs={{0,32},{1,33},{2,34},{3,35},{4,36},{5,37},{6,38},{7,39},{8,40},{9,... | collective-permute-start | bytes 1572872 | tf_op jit(solution)/shard_map/ppermute | solution.py:242
  54.0 59.5 %collective-permute-start.1 = (bf16[8,2,128,128]{3,2,1,0:T(8,128)(2,1)}, bf16[8,2,128,128]{3,2,1,0:T(8,128)(2,1)}, u32[]{:S(2)}, u32[]{:S(2)}) collective-permute-start(bf16[8,2,128,128]{3,2,1,0:T(8,128)(2,1)} %get-tuple-element.17), channel_id=1, source_target_pairs={{0,16},{1,17},{2,18},{3,19},{4,20},{5,21},{6,22},{7,23},{8,24},{9,... | collective-permute-start | bytes 1572872 | tf_op jit(solution)/shard_map/ppermute | solution.py:242
  56.2 57.3 %collective-permute-start = (bf16[8,2,128,128]{3,2,1,0:T(8,128)(2,1)}, bf16[8,2,128,128]{3,2,1,0:T(8,128)(2,1)}, u32[]{:S(2)}, u32[]{:S(2)}) collective-permute-start(bf16[8,2,128,128]{3,2,1,0:T(8,128)(2,1)} %get-tuple-element.17), channel_id=1, source_target_pairs={{0,32},{1,33},{2,34},{3,35},{4,36},{5,37},{6,38},{7,39},{8,40},{9,... | collective-permute-start | bytes 1572872 | tf_op jit(solution)/shard_map/ppermute | solution.py:242
  61.5 42.2 %all-to-all-start.1 = ((bf16[16,2,128,128]{3,2,1,0:T(8,128)(2,1)}), bf16[16,2,128,128]{3,2,1,0:T(8,128)(2,1)S(1)}, u32[]{:S(2)}, u32[]{:S(2)}) async-start(bf16[16,2,128,128]{3,2,1,0:T(8,128)(2,1)} %get-tuple-element.10), calls=%async_computation.1 | async-start | bytes 2097152 | tf_op jit(solution)/shard_map/all_to_all | solution.py:246
  103.7 43.3 %all-to-all-start.4 = ((bf16[16,4,128,128]{3,2,1,0:T(8,128)(2,1)}), bf16[16,4,128,128]{3,2,1,0:T(8,128)(2,1)S(1)}, u32[]{:S(2)}, u32[]{:S(2)}) async-start(bf16[16,4,128,128]{3,2,1,0:T(8,128)(2,1)} %attention.3), calls=%async_computation.4 | async-start | bytes 4194304 | tf_op jit(solution)/shard_map/all_to_all | solution.py:246
  147.0 1.3 copy-start
  148.4 35.9 %all-to-all-start.2 = ((bf16[16,4,128,128]{3,2,1,0:T(8,128)(2,1)}), bf16[16,4,128,128]{3,2,1,0:T(8,128)(2,1)S(1)}, u32[]{:S(2)}, u32[]{:S(2)}) async-start(bf16[16,4,128,128]{3,2,1,0:T(8,128)(2,1)} %attention.2), calls=%async_computation.2 | async-start | bytes 4194304 | tf_op jit(solution)/shard_map/all_to_all | solution.py:246
  155.6 1.6 copy-start.1
